TPU v7x, 32 devices: a whole 2x2x4 slice. The times are simulated.
32 devices in a mesh: energy: 8 (over z, core), momentum: 4 (over y, x).
Axes of the slice: x: 2, y: 2, z: 4, core: 2. Of those that a mesh axis runs over, the one named last changes fastest.
Arguments:
- green: bfloat16 [24, 4, 2, 384, 384], P('energy', 'momentum'), may hold values from -0.3125 to 0.3125
- contact: bfloat16 [24, 4, 2, 3, 128, 128], P('energy', 'momentum'), may hold values from -6 to 6
- tile_count: int32 [24], P('energy'), may hold values from 1 to 3
- offsets: int32 [3], replicated, may hold values from 1 to 3, as said below
- pair_index: int32 [3, 4, 4], replicated, may hold values from 0 to 15
- coupling_table: float32 [3, 16], replicated, may hold values from 0.05 to 0.3
Outputs:
- lesser_tiles: bfloat16 [24, 4, 2, 3, 128, 128], P('energy', 'momentum')
- self_energy: bfloat16 [24, 4, 2, 3, 128, 128], P('energy', 'momentum')
Inputs may be any that keep to these rules, and one draw needn't show every extreme that they name: `offsets`: the largest offset equals 3 in every draw.
All inputs are finite; a program needn't handle non-finite values.
Results may differ from a plain program's by a relative error of at most 0.009.
Values may be sent and summed in bfloat16 or wider, within the bound.
A program may use at most 64 MiB of HBM per device.

v0:
```python
import jax
import jax.numpy as jnp
from jax import lax
from jax.sharding import PartitionSpec as P

OMAX = 3
ITERS = 2


def padded_2(block, sides, width):
    for axis, dim in sides:
        count = lax.axis_size(axis)
        forward = [(i, i + 1) for i in range(count - 1)]
        backward = [(target, source) for source, target in forward]
        low = lax.ppermute(
            lax.slice_in_dim(block, block.shape[dim] - width, None, axis=dim), axis, forward
        )
        high = lax.ppermute(lax.slice_in_dim(block, 0, width, axis=dim), axis, backward)
        block = jnp.concatenate([low, block, high], axis=dim)
    return block


def couplings(pair_index, coupling_table, count_table):
    hits = (pair_index[..., None] == jnp.arange(count_table, dtype=jnp.int32)).astype(jnp.float32)
    return jnp.einsum("mkqc,mc->mkq", hits, coupling_table, precision=lax.Precision.HIGHEST)


def lesser_onsite(blocks, sigma, counts):
    energies, order = (blocks.shape[0], blocks.shape[-1])
    tiles, width = (sigma.shape[2], sigma.shape[3])
    g_real = blocks[:, 0].reshape(energies, order, tiles, width)
    g_imag = blocks[:, 1].reshape(energies, order, tiles, width)
    s_real = sigma[:, 0]
    s_imag = sigma[:, 1]
    form = "ertc,etcd->ertd"
    polarization_real = jnp.einsum(
        form, g_real, s_real, preferred_element_type=jnp.float32
    ) - jnp.einsum(form, g_imag, s_imag, preferred_element_type=jnp.float32)
    polarization_imag = jnp.einsum(
        form, g_real, s_imag, preferred_element_type=jnp.float32
    ) + jnp.einsum(form, g_imag, s_real, preferred_element_type=jnp.float32)
    polarization_real = polarization_real.astype(jnp.bfloat16).reshape(
        energies, tiles, width, order
    )
    polarization_imag = polarization_imag.astype(jnp.bfloat16).reshape(
        energies, tiles, width, order
    )
    hamiltonian_real = blocks[:, 0].reshape(energies, tiles, width, order)
    hamiltonian_imag = blocks[:, 1].reshape(energies, tiles, width, order)
    pairs = "etab,etcb->etac"
    phonon_propagator_real = jnp.einsum(
        pairs, polarization_real, hamiltonian_real, preferred_element_type=jnp.float32
    ) + jnp.einsum(pairs, polarization_imag, hamiltonian_imag, preferred_element_type=jnp.float32)
    phonon_propagator_imag = jnp.einsum(
        pairs, polarization_imag, hamiltonian_real, preferred_element_type=jnp.float32
    ) - jnp.einsum(pairs, polarization_real, hamiltonian_imag, preferred_element_type=jnp.float32)
    live = (jnp.arange(tiles, dtype=jnp.int32)[None, :] < counts[:, None]).astype(jnp.float32)[
        :, :, None, None
    ]
    return jnp.stack([phonon_propagator_real * live, phonon_propagator_imag * live], axis=1).astype(
        jnp.bfloat16
    )


def body(green, contact, tile_count, offsets, pair_index, coupling_table):
    energies = green.shape[0]
    modes = offsets.shape[0]
    coupling = couplings(pair_index, coupling_table, coupling_table.shape[1])
    sigma = contact
    lesser = contact
    for sweep in range(ITERS):
        lesser = lesser_onsite(green[:, 0], sigma[:, 0], tile_count)[:, None]
        total = contact.astype(jnp.float32)
        padded = padded_2(lesser, (("energy", 0),), OMAX)
        banded_coupling = lax.all_to_all(
            padded, "momentum", split_axis=4, concat_axis=1, tiled=True
        )
        widened = banded_coupling.astype(jnp.float32)
        band_sum = jnp.zeros((energies,) + widened.shape[1:], jnp.float32)
        for phonon_mode in range(modes):
            mixed = jnp.einsum(
                "kq,eqabcd->ekabcd", coupling[phonon_mode], widened, precision=lax.Precision.HIGHEST
            )
            shift = offsets[phonon_mode]
            lower = lax.dynamic_slice_in_dim(mixed, OMAX - shift, energies, 0)
            upper = lax.dynamic_slice_in_dim(mixed, OMAX + shift, energies, 0)
            band_sum = band_sum + (lower + upper)
        phonon = lax.all_to_all(band_sum, "momentum", split_axis=1, concat_axis=4, tiled=True)
        total = total + phonon
        sigma = total.astype(jnp.bfloat16)
    return (lesser, sigma)


def solution(mesh):
    in_specs = (
        P("energy", "momentum", None, None, None),
        P("energy", "momentum", None, None, None, None),
        P("energy"),
        P(),
        P(),
        P(),
    )
    out_specs = (
        P("energy", "momentum", None, None, None, None),
        P("energy", "momentum", None, None, None, None),
    )
    return jax.shard_map(body, mesh=mesh, in_specs=in_specs, out_specs=out_specs, check_vma=False)
```

profile of v0, /device:TPU:9, one launch (start us, length us, event | category | flops | bytes accessed | tf_op | source)
XLA Modules:
  0.0 212.1 jit_solution(2933771193482233110)
XLA Ops:
  0.6 2.8 %copy.108 = bf16[3,1,2,384,384]{3,4,0,2,1:T(8,128)(2,1)S(1)} copy(bf16[3,1,2,384,384]{4,3,2,1,0:T(8,128)(2,1)} %param.6) | data formatting | bytes 3538944 | tf_op args[0]
  3.6 1.4 copy.106
  5.0 2.4 %copy.112 = bf16[3,1,384,384]{3,2,0,1:T(8,128)(2,1)S(1)} copy(bf16[3,1,384,384]{2,3,0,1:T(8,128)(2,1)S(1)} %get-tuple-element.13) | data formatting | bytes 1769472 | tf_op jit(solution)/shard_map/slice | solution.py:31
  7.4 1.6 fusion.37
  9.0 1.6 fusion.38
  10.6 2.3 %copy.116 = bf16[3,1,384,384]{3,2,0,1:T(8,128)(2,1)S(1)} copy(bf16[3,1,384,384]{2,3,0,1:T(8,128)(2,1)S(1)} %get-tuple-element.12) | data formatting | bytes 1769472 | tf_op jit(solution)/shard_map/slice | solution.py:32
  13.0 3.2 %fusion.12 = bf16[3,384,3,128]{1,3,2,0:T(8,128)(2,1)} fusion(f32[3,3,128,384]{3,2,1,0:T(8,128)} %fusion.37, bf16[3,384,3,128]{1,3,2,0:T(8,128)(2,1)S(1)} %bitcast.158, bf16[3,2,3,128,128]{3,4,2,0,1:T(8,128)(2,1)} %bitcast.178), kind=kOutput, calls=%fused_computation.20 | convolution fusion | flops 114130944 | bytes 3833856 | tf_op jit(solution)/shard_map/ertc,etcd->ertd/dot_general | solution.py:38
  16.2 3.4 %reshape.138 = bf16[3,3,128,384]{2,1,3,0:T(4,128)(2,1)} reshape(bf16[3,384,3,128]{1,3,2,0:T(8,128)(2,1)} %fusion.12) | data formatting | bytes 1769472 | tf_op jit(solution)/shard_map/reshape | solution.py:42
  19.6 3.2 %copy.150 = bf16[3,3,128,384]{3,2,1,0:T(8,128)(2,1)} copy(bf16[3,3,128,384]{2,1,3,0:T(4,128)(2,1)} %reshape.138) | data formatting | bytes 1769472 | tf_op jit(solution)/shard_map/reshape | solution.py:42
  22.9 2.9 %fusion.13 = bf16[3,384,3,128]{1,3,2,0:T(8,128)(2,1)} fusion(f32[3,3,128,384]{3,2,1,0:T(8,128)} %fusion.38, bf16[3,384,3,128]{1,3,2,0:T(8,128)(2,1)S(1)} %bitcast.159, bf16[3,2,3,128,128]{3,4,2,0,1:T(8,128)(2,1)} %bitcast.179), kind=kOutput, calls=%fused_computation.21 | convolution fusion | flops 114130944 | bytes 3833856 | tf_op jit(solution)/shard_map/ertc,etcd->ertd/dot_general | solution.py:41
  25.8 3.4 %reshape.139 = bf16[3,3,128,384]{2,1,3,0:T(4,128)(2,1)} reshape(bf16[3,384,3,128]{1,3,2,0:T(8,128)(2,1)} %fusion.13) | data formatting | bytes 1769472 | tf_op jit(solution)/shard_map/reshape | solution.py:45
  29.2 3.2 %copy.151 = bf16[3,3,128,384]{3,2,1,0:T(8,128)(2,1)} copy(bf16[3,3,128,384]{2,1,3,0:T(4,128)(2,1)} %reshape.139) | data formatting | bytes 1769472 | tf_op jit(solution)/shard_map/reshape | solution.py:45
  32.5 1.7 fusion.47
  36.5 3.8 %collective-permute-start = (bf16[3,1,2,3,128,128]{5,4,3,0,2,1:T(8,128)(2,1)S(1)}, bf16[3,1,2,3,128,128]{5,4,3,0,2,1:T(8,128)(2,1)S(1)}, u32[]{:S(2)}, u32[]{:S(2)}) collective-permute-start(bf16[3,1,2,3,128,128]{5,4,3,0,2,1:T(8,128)(2,1)S(1)} %pad_maximum_fusion.2), channel_id=1, source_target_pairs={{0,4},{4,8},{8,12},{12,16},{16,20},{20,24},{24,28},{1,5},{5,9},{9,... | collective-permute-start | bytes 1769480 | tf_op jit(solution)/shard_map/ppermute | solution.py:15
  40.3 1.9 collective-permute-start.1
  42.2 4.9 %collective-permute-done = bf16[3,1,2,3,128,128]{5,4,3,0,2,1:T(8,128)(2,1)S(1)} collective-permute-done((bf16[3,1,2,3,128,128]{5,4,3,0,2,1:T(8,128)(2,1)S(1)}, bf16[3,1,2,3,128,128]{5,4,3,0,2,1:T(8,128)(2,1)S(1)}, u32[]{:S(2)}, u32[]{:S(2)}) %collective-permute-start) | collective-permute-done | bytes 589856 | tf_op jit(solution)/shard_map/ppermute | solution.py:15
  47.1 4.4 %collective-permute-done.1 = bf16[3,1,2,3,128,128]{5,4,3,0,2,1:T(8,128)(2,1)S(1)} collective-permute-done((bf16[3,1,2,3,128,128]{5,4,3,0,2,1:T(8,128)(2,1)S(1)}, bf16[3,1,2,3,128,128]{5,4,3,0,2,1:T(8,128)(2,1)S(1)}, u32[]{:S(2)}, u32[]{:S(2)}) %collective-permute-start.1) | collective-permute-done | bytes 589856 | tf_op jit(solution)/shard_map/ppermute | solution.py:18
  51.7 3.1 %copy.117 = bf16[9,1,2,3,128,128]{5,2,3,1,0,4:T(2,128)(2,1)} copy(bf16[9,1,2,3,128,128]{5,4,3,0,2,1:T(8,128)(2,1)S(1)} %pad_maximum_fusion) | data formatting | bytes 3538944 | tf_op jit(solution)/shard_map/concatenate | solution.py:19
  54.8 3.9 %all-to-all-start = ((bf16[9,1,2,3,128,128]{5,2,3,1,0,4:T(2,128)(2,1)}), bf16[9,1,2,3,128,128]{5,2,3,1,0,4:T(2,128)(2,1)S(1)}, u32[]{:S(2)}, u32[]{:S(2)}) async-start(bf16[9,1,2,3,128,128]{5,2,3,1,0,4:T(2,128)(2,1)} %copy.117), calls=%async_computation | async-start | bytes 3538944 | tf_op jit(solution)/shard_map/all_to_all | solution.py:75
  68.3 11.1 %all-to-all-done = bf16[9,1,2,3,128,128]{5,2,3,1,0,4:T(2,128)(2,1)S(1)} async-done(((bf16[9,1,2,3,128,128]{5,2,3,1,0,4:T(2,128)(2,1)}), bf16[9,1,2,3,128,128]{5,2,3,1,0,4:T(2,128)(2,1)S(1)}, u32[]{:S(2)}, u32[]{:S(2)}) %all-to-all-start) | async-done | bytes 1769504 | tf_op jit(solution)/shard_map/all_to_all | solution.py:75
  79.4 4.4 %fusion.10 = f32[9,2,3,32,128,4]{4,5,3,2,1,0:T(4,128)S(1)} fusion(bf16[9,1,2,3,4,32,128]{6,2,3,0,5,4,1:T(2,128)(2,1)S(1)} %bitcast.162, f32[3,4,4]{2,1,0:T(4,128)S(1)} %bitcast.183), kind=kOutput, calls=%fused_computation.12 | convolution fusion | flops 42467328 | bytes 5310464 | tf_op jit(solution)/shard_map/kq,eqabcd->ekabcd/dot_general | solution.py:81
  83.8 4.4 %fusion.6 = f32[9,2,3,32,128,4]{4,5,3,2,1,0:T(4,128)S(1)} fusion(bf16[9,1,2,3,4,32,128]{6,2,3,0,5,4,1:T(2,128)(2,1)S(1)} %bitcast.163, f32[3,4,4]{2,1,0:T(4,128)S(1)} %bitcast.184), kind=kOutput, calls=%fused_computation.8 | convolution fusion | flops 42467328 | bytes 5310464 | tf_op jit(solution)/shard_map/kq,eqabcd->ekabcd/dot_general | solution.py:81
  88.2 4.4 %fusion.8 = f32[9,2,3,32,128,4]{4,5,3,2,1,0:T(4,128)S(1)} fusion(bf16[9,1,2,3,4,32,128]{6,2,3,0,5,4,1:T(2,128)(2,1)S(1)} %bitcast.164, f32[3,4,4]{2,1,0:T(4,128)S(1)} %bitcast.185), kind=kOutput, calls=%fused_computation.10 | convolution fusion | flops 42467328 | bytes 5310464 | tf_op jit(solution)/shard_map/kq,eqabcd->ekabcd/dot_general | solution.py:81
  92.6 1.3 add_bitcast_fusion.1
  94.0 17.4 %all_to_all.72 = f32[3,4,2,3,32,128]{5,4,3,2,0,1:T(8,128)S(1)} all-to-all(f32[3,4,2,3,32,128]{5,4,3,2,0,1:T(8,128)S(1)} %copy.120), channel_id=1, replica_groups=mesh['energy'=8,'momentum'=4] {'momentum'}, dimensions={1} | all-to-all | bytes 2359296 | tf_op jit(solution)/shard_map/all_to_all | solution.py:88
  111.6 1.4 copy.122
  113.0 1.4 fusion.36
  114.8 1.7 fusion.40
  116.9 1.7 reshape.140
  118.6 2.5 %copy.154 = bf16[3,3,128,384]{3,2,1,0:T(8,128)(2,1)S(1)} copy(bf16[3,3,128,384]{2,1,3,0:T(4,128)(2,1)} %reshape.140) | data formatting | bytes 1769472 | tf_op jit(solution)/shard_map/reshape | solution.py:42
  121.2 1.3 fusion.49
  123.0 1.3 fusion.15
  124.3 3.4 %reshape.141 = bf16[3,3,128,384]{2,1,3,0:T(4,128)(2,1)} reshape(bf16[3,384,3,128]{1,3,2,0:T(8,128)(2,1)} %fusion.15) | data formatting | bytes 1769472 | tf_op jit(solution)/shard_map/reshape | solution.py:45
  127.7 3.3 %copy.155 = bf16[3,3,128,384]{3,2,1,0:T(8,128)(2,1)} copy(bf16[3,3,128,384]{2,1,3,0:T(4,128)(2,1)} %reshape.141) | data formatting | bytes 1769472 | tf_op jit(solution)/shard_map/reshape | solution.py:45
  131.0 1.8 fusion.50
  134.0 4.6 %collective-permute-start.2 = (bf16[3,1,2,3,128,128]{5,4,3,0,2,1:T(8,128)(2,1)S(1)}, bf16[3,1,2,3,128,128]{5,4,3,0,2,1:T(8,128)(2,1)S(1)}, u32[]{:S(2)}, u32[]{:S(2)}) collective-permute-start(bf16[3,1,2,3,128,128]{5,4,3,0,2,1:T(8,128)(2,1)S(1)} %pad_maximum_fusion.3), channel_id=1, source_target_pairs={{0,4},{4,8},{8,12},{12,16},{16,20},{20,24},{24,28},{1,5},{5,9},{9,... | collective-permute-start | bytes 1769480 | tf_op jit(solution)/shard_map/ppermute | solution.py:15
  138.6 1.9 collective-permute-start.3
  140.5 4.9 %collective-permute-done.2 = bf16[3,1,2,3,128,128]{5,4,3,0,2,1:T(8,128)(2,1)S(1)} collective-permute-done((bf16[3,1,2,3,128,128]{5,4,3,0,2,1:T(8,128)(2,1)S(1)}, bf16[3,1,2,3,128,128]{5,4,3,0,2,1:T(8,128)(2,1)S(1)}, u32[]{:S(2)}, u32[]{:S(2)}) %collective-permute-start.2) | collective-permute-done | bytes 589856 | tf_op jit(solution)/shard_map/ppermute | solution.py:15
  145.4 4.4 %collective-permute-done.3 = bf16[3,1,2,3,128,128]{5,4,3,0,2,1:T(8,128)(2,1)S(1)} collective-permute-done((bf16[3,1,2,3,128,128]{5,4,3,0,2,1:T(8,128)(2,1)S(1)}, bf16[3,1,2,3,128,128]{5,4,3,0,2,1:T(8,128)(2,1)S(1)}, u32[]{:S(2)}, u32[]{:S(2)}) %collective-permute-start.3) | collective-permute-done | bytes 589856 | tf_op jit(solution)/shard_map/ppermute | solution.py:18
  150.0 1.8 copy.129
  151.8 23.9 %all_to_all.73 = bf16[9,1,2,3,128,128]{5,2,3,1,0,4:T(2,128)(2,1)S(1)} all-to-all(bf16[9,1,2,3,128,128]{5,2,3,1,0,4:T(2,128)(2,1)S(1)} %copy.129), channel_id=1, replica_groups=mesh['energy'=8,'momentum'=4] {'momentum'}, dimensions={4} | all-to-all | bytes 3538944 | tf_op jit(solution)/shard_map/all_to_all | solution.py:75
  175.7 4.4 %fusion.2 = f32[9,2,3,32,128,4]{4,5,3,2,1,0:T(4,128)S(1)} fusion(bf16[9,1,2,3,4,32,128]{6,2,3,0,5,4,1:T(2,128)(2,1)S(1)} %bitcast.165, f32[3,4,4]{2,1,0:T(4,128)S(1)} %bitcast.186), kind=kOutput, calls=%fused_computation.4 | convolution fusion | flops 42467328 | bytes 5310464 | tf_op jit(solution)/shard_map/kq,eqabcd->ekabcd/dot_general | solution.py:81
  180.1 4.4 %fusion.4 = f32[9,2,3,32,128,4]{4,5,3,2,1,0:T(4,128)S(1)} fusion(bf16[9,1,2,3,4,32,128]{6,2,3,0,5,4,1:T(2,128)(2,1)S(1)} %bitcast.166, f32[3,4,4]{2,1,0:T(4,128)S(1)} %bitcast.187), kind=kOutput, calls=%fused_computation.6 | convolution fusion | flops 42467328 | bytes 5310464 | tf_op jit(solution)/shard_map/kq,eqabcd->ekabcd/dot_general | solution.py:81
  184.5 4.4 %fusion = f32[9,2,3,32,128,4]{4,5,3,2,1,0:T(4,128)S(1)} fusion(bf16[9,1,2,3,4,32,128]{6,2,3,0,5,4,1:T(2,128)(2,1)S(1)} %bitcast.167, f32[3,4,4]{2,1,0:T(4,128)S(1)} %bitcast.188), kind=kOutput, calls=%fused_computation.2 | convolution fusion | flops 42467328 | bytes 5310464 | tf_op jit(solution)/shard_map/kq,eqabcd->ekabcd/dot_general | solution.py:81
  188.9 1.3 add_bitcast_fusion
  190.1 1.2 copy.132
  191.4 3.5 %all-to-all-start.3 = ((f32[3,4,2,3,32,128]{5,4,3,2,0,1:T(8,128)}), f32[3,4,2,3,32,128]{5,4,3,2,0,1:T(8,128)S(1)}, u32[]{:S(2)}, u32[]{:S(2)}) async-start(f32[3,4,2,3,32,128]{5,4,3,2,0,1:T(8,128)} %copy.132), calls=%async_computation.3 | async-start | bytes 2359296 | tf_op jit(solution)/shard_map/all_to_all | solution.py:88
  195.7 14.6 %all-to-all-done.3 = f32[3,4,2,3,32,128]{5,4,3,2,0,1:T(8,128)S(1)} async-done(((f32[3,4,2,3,32,128]{5,4,3,2,0,1:T(8,128)}), f32[3,4,2,3,32,128]{5,4,3,2,0,1:T(8,128)S(1)}, u32[]{:S(2)}, u32[]{:S(2)}) %all-to-all-start.3) | async-done | bytes 1179680 | tf_op jit(solution)/shard_map/all_to_all | solution.py:88
  (56 shorter events, 10.0 us)
Async XLA Ops:
  0.6 66.4 %copy-start = (f32[3,16]{1,0:T(4,128)S(1)}, f32[3,16]{1,0:T(4,128)}, u32[]{:S(2)}) copy-start(f32[3,16]{1,0:T(4,128)} %param.11) | copy-start | bytes 580
  5.0 4.0 %copy-start.6 = (bf16[3,1,2,3,128,128]{4,5,3,0,2,1:T(8,128)(2,1)}, bf16[3,1,2,3,128,128]{4,5,3,0,2,1:T(8,128)(2,1)S(1)}, u32[]{:S(2)}) copy-start(bf16[3,1,2,3,128,128]{4,5,3,0,2,1:T(8,128)(2,1)S(1)} %copy.106) | copy-start | bytes 1769476
  7.4 26.9 %copy-start.4 = (bf16[3,1,384,384]{3,2,0,1:T(8,128)(2,1)}, bf16[3,1,384,384]{3,2,0,1:T(8,128)(2,1)S(1)}, u32[]{:S(2)}) copy-start(bf16[3,1,384,384]{3,2,0,1:T(8,128)(2,1)S(1)} %copy.112) | copy-start | bytes 2654212
  13.0 22.3 %copy-start.2 = (bf16[3,1,384,384]{3,2,0,1:T(8,128)(2,1)}, bf16[3,1,384,384]{3,2,0,1:T(8,128)(2,1)S(1)}, u32[]{:S(2)}) copy-start(bf16[3,1,384,384]{3,2,0,1:T(8,128)(2,1)S(1)} %copy.116) | copy-start | bytes 2654212
  25.8 6.7 %copy-start.16 = (s32[3]{0:T(128)S(1)}, s32[3]{0:T(128)}, u32[]{:S(2)}) copy-start(s32[3]{0:T(128)} %param.8) | copy-start | bytes 40
  32.4 1.8 copy-start.9
  34.8 1.2 copy-start.8
  36.5 10.6 %collective-permute-start = (bf16[3,1,2,3,128,128]{5,4,3,0,2,1:T(8,128)(2,1)S(1)}, bf16[3,1,2,3,128,128]{5,4,3,0,2,1:T(8,128)(2,1)S(1)}, u32[]{:S(2)}, u32[]{:S(2)}) collective-permute-start(bf16[3,1,2,3,128,128]{5,4,3,0,2,1:T(8,128)(2,1)S(1)} %pad_maximum_fusion.2), channel_id=1, source_target_pairs={{0,4},{4,8},{8,12},{12,16},{16,20},{20,24},{24,28},{1,5},{5,9},{9,... | collective-permute-start | bytes 1769480 | tf_op jit(solution)/shard_map/ppermute | solution.py:15
  40.3 11.2 %collective-permute-start.1 = (bf16[3,1,2,3,128,128]{5,4,3,0,2,1:T(8,128)(2,1)S(1)}, bf16[3,1,2,3,128,128]{5,4,3,0,2,1:T(8,128)(2,1)S(1)}, u32[]{:S(2)}, u32[]{:S(2)}) collective-permute-start(bf16[3,1,2,3,128,128]{5,4,3,0,2,1:T(8,128)(2,1)S(1)} %pad_maximum_fusion.2), channel_id=1, source_target_pairs={{4,0},{8,4},{12,8},{16,12},{20,16},{24,20},{28,24},{5,1},{9,5},{13... | collective-permute-start | bytes 1769480 | tf_op jit(solution)/shard_map/ppermute | solution.py:18
  54.8 3.9 %copy-start.15 = (s32[3]{0:T(128)S(1)}, s32[3]{0:T(128)}, u32[]{:S(2)}) copy-start(s32[3]{0:T(128)} %param.9) | copy-start | bytes 40
  54.8 24.6 %all-to-all-start = ((bf16[9,1,2,3,128,128]{5,2,3,1,0,4:T(2,128)(2,1)}), bf16[9,1,2,3,128,128]{5,2,3,1,0,4:T(2,128)(2,1)S(1)}, u32[]{:S(2)}, u32[]{:S(2)}) async-start(bf16[9,1,2,3,128,128]{5,2,3,1,0,4:T(2,128)(2,1)} %copy.117), calls=%async_computation | async-start | bytes 3538944 | tf_op jit(solution)/shard_map/all_to_all | solution.py:75
  111.5 1.4 copy-start.7
  114.4 2.1 copy-start.12
  116.9 4.2 %copy-start.5 = (bf16[3,1,384,384]{3,2,0,1:T(8,128)(2,1)S(1)}, bf16[3,1,384,384]{3,2,0,1:T(8,128)(2,1)}, u32[]{:S(2)}) copy-start(bf16[3,1,384,384]{3,2,0,1:T(8,128)(2,1)} %copy-done.4) | copy-start | bytes 2654212
  121.2 1.5 copy-start.11
  121.2 1.8 copy-start.13
  127.7 5.1 %copy-start.3 = (bf16[3,1,384,384]{3,2,0,1:T(8,128)(2,1)S(1)}, bf16[3,1,384,384]{3,2,0,1:T(8,128)(2,1)}, u32[]{:S(2)}) copy-start(bf16[3,1,384,384]{3,2,0,1:T(8,128)(2,1)} %copy-done.2) | copy-start | bytes 2654212
  131.0 1.8 copy-start.10
  131.0 1.8 copy-start.14
  134.0 11.4 %collective-permute-start.2 = (bf16[3,1,2,3,128,128]{5,4,3,0,2,1:T(8,128)(2,1)S(1)}, bf16[3,1,2,3,128,128]{5,4,3,0,2,1:T(8,128)(2,1)S(1)}, u32[]{:S(2)}, u32[]{:S(2)}) collective-permute-start(bf16[3,1,2,3,128,128]{5,4,3,0,2,1:T(8,128)(2,1)S(1)} %pad_maximum_fusion.3), channel_id=1, source_target_pairs={{0,4},{4,8},{8,12},{12,16},{16,20},{20,24},{24,28},{1,5},{5,9},{9,... | collective-permute-start | bytes 1769480 | tf_op jit(solution)/shard_map/ppermute | solution.py:15
  138.6 11.2 %collective-permute-start.3 = (bf16[3,1,2,3,128,128]{5,4,3,0,2,1:T(8,128)(2,1)S(1)}, bf16[3,1,2,3,128,128]{5,4,3,0,2,1:T(8,128)(2,1)S(1)}, u32[]{:S(2)}, u32[]{:S(2)}) collective-permute-start(bf16[3,1,2,3,128,128]{5,4,3,0,2,1:T(8,128)(2,1)S(1)} %pad_maximum_fusion.3), channel_id=1, source_target_pairs={{4,0},{8,4},{12,8},{16,12},{20,16},{24,20},{28,24},{5,1},{9,5},{13... | collective-permute-start | bytes 1769480 | tf_op jit(solution)/shard_map/ppermute | solution.py:18
  191.4 19.0 %all-to-all-start.3 = ((f32[3,4,2,3,32,128]{5,4,3,2,0,1:T(8,128)}), f32[3,4,2,3,32,128]{5,4,3,2,0,1:T(8,128)S(1)}, u32[]{:S(2)}, u32[]{:S(2)}) async-start(f32[3,4,2,3,32,128]{5,4,3,2,0,1:T(8,128)} %copy.132), calls=%async_computation.3 | async-start | bytes 2359296 | tf_op jit(solution)/shard_map/all_to_all | solution.py:88
  210.5 1.6 copy-start.1
where the time goes:
time: 213 us; the launch traced here: 212 us
  matrix products  48.1 us (23%)
  local copies, waits for them, and re-layouts  45.3 us (21%)
  waiting for transfers between devices  44.3 us (21%)
  blocking collectives  41.3 us (19%)
  starting transfers between devices  19.6 us (9%)
  between operations  8.81 us (4%)
  other arithmetic  4.69 us (2%)
    dot_general x6, matrix products, body(): jnp.einsum('kq,eqabcd->ekabcd', coupling[phonon_mode], widened, precision...  26.4 us
    all_to_all x1, blocking collectives, body(): lax.all_to_all(padded, 'momentum', split_axis=4, concat_axis=1, tiled=True)  23.9 us
    all_to_all x1, blocking collectives, body(): lax.all_to_all(band_sum, 'momentum', split_axis=1, concat_axis=4, tiled=T...  17.4 us
    all_to_all x1, waiting for transfers between devices, body(): lax.all_to_all(band_sum, 'momentum', split_axis=1, concat_axis=4, tiled=T...  14.6 us
    reshape x4, local copies, waits for them, and re-layouts, lesser_onsite(): polarization_imag.astype(jnp.bfloat16)  13.4 us
    all_to_all x1, waiting for transfers between devices, body(): lax.all_to_all(padded, 'momentum', split_axis=4, concat_axis=1, tiled=True)  11.1 us
    reshape x4, local copies, waits for them, and re-layouts, lesser_onsite(): polarization_real.astype(jnp.bfloat16)  10.9 us
    ppermute x2, waiting for transfers between devices, padded_2(): lax.ppermute(lax.slice_in_dim(block, block.shape[dim] - width, None, axis...  9.75 us
  transfers between devices with their start and end apart: 6, of which 6 were waited for; matrix products, arithmetic and copies ran while one was open for 1% of the time, Pallas kernels for 0%

commit v1 on v0

v1 whole, which is shorter than its diff:
```python
import functools

import jax
import jax.numpy as jnp
from jax import lax
from jax.experimental import pallas as pl
from jax.experimental.pallas import tpu as pltpu
from jax.sharding import PartitionSpec as P

OMAX = 3
ITERS = 2
PACK = 16
CHUNKS = 3
MESH = pl.DeviceIdType.MESH


def born(ne, nk, chunks, green, contact, counts, offsets, pairs, table, lesser_out, sigma_out,
         g, start, product, lesser, band, mixed, back, sigma, weights,
         in_sem, own_sem, out_sem, a_send, a_recv, h_send, h_recv, b_send, b_recv):
    energies, order = g.shape[0], g.shape[-1]
    tile = start.shape[-1]
    tiles = order // tile
    rows = band.shape[4]
    part = rows // chunks
    modes = offsets.shape[0]
    e, me = lax.axis_index("energy"), lax.axis_index("momentum")
    has_left, has_right = e > 0, e < ne - 1
    left, right = jnp.maximum(e - 1, 0), jnp.minimum(e + 1, ne - 1)

    loads = [pltpu.make_async_copy(contact, start, in_sem.at[energies])]
    loads += [pltpu.make_async_copy(green.at[i], g.at[i], in_sem.at[i]) for i in range(energies)]
    for load in loads:
        load.start()

    def peer(j):
        return lax.rem(me + j, nk)

    barrier = pltpu.get_barrier_semaphore()
    for j in range(1, nk):
        pl.semaphore_signal(barrier, inc=1, device_id={"momentum": peer(j)}, device_id_type=MESH)

    @pl.when(has_left)
    def _():
        pl.semaphore_signal(barrier, inc=1, device_id={"energy": left}, device_id_type=MESH)

    @pl.when(has_right)
    def _():
        pl.semaphore_signal(barrier, inc=1, device_id={"energy": right}, device_id_type=MESH)

    def weigh(i, carry):
        k, q = i // nk, i % nk
        sums = [jnp.float32(0)] * OMAX
        for m in range(modes):
            value = table[m, pairs[m, k, q]]
            for d in range(OMAX):
                sums[d] = sums[d] + jnp.where(offsets[m] == d + 1, value, jnp.float32(0))
        for d in range(OMAX):
            weights[d, k, q] = jnp.full(weights.shape[3:], sums[d], jnp.float32)
        return carry

    lax.fori_loop(0, nk * nk, weigh, 0)

    def clear(side):
        for it in range(ITERS):
            for i in range(energies):
                def zero(q, carry):
                    band[it, side, i, q] = jnp.zeros(band.shape[4:], band.dtype)
                    return carry
                lax.fori_loop(0, nk, zero, 0)

    @pl.when(e == 0)
    def _():
        clear(0)

    @pl.when(e == ne - 1)
    def _():
        clear(2)

    def onsite(it, i, source):
        for t in range(tiles):
            cols = slice(t * tile, (t + 1) * tile)
            s_real = source[i, t * tile:(t + 1) * tile, :]
            s_imag = source[i, (tiles + t) * tile:(tiles + t + 1) * tile, :]
            s = jnp.concatenate([jnp.concatenate([s_real, s_imag], 1),
                                 jnp.concatenate([-s_imag, s_real], 1)], 0)
            a = jnp.concatenate([g[i, 0, :, cols], g[i, 1, :, cols]], 1)
            p = jnp.dot(a, s, preferred_element_type=jnp.float32).astype(jnp.bfloat16)
            product[0, :, cols] = p[:, :tile]
            product[1, :, cols] = p[:, tile:]
        for t in range(tiles):
            r = slice(t * tile, (t + 1) * tile)
            p = jnp.concatenate([product[0, r, :], product[1, r, :]], 0)
            h = jnp.concatenate([g[i, 0, r, :], g[i, 1, r, :]], 0)
            o = lax.dot_general(p, h, (((1,), (1,)), ((), ())), preferred_element_type=jnp.float32)
            live = jnp.where(t < counts[i], jnp.float32(1), jnp.float32(0))
            real = (o[:tile, :tile] + o[tile:, tile:]) * live
            imag = (o[tile:, :tile] - o[:tile, tile:]) * live
            lesser[it, i, t * tile:(t + 1) * tile, :] = real.astype(jnp.bfloat16)
            lesser[it, i, (tiles + t) * tile:(tiles + t + 1) * tile, :] = imag.astype(jnp.bfloat16)

    def span(owner, c):
        return pl.ds(pl.multiple_of(owner * rows + c * part, PACK), part)

    def outward(it, c, j):
        return pltpu.make_async_remote_copy(
            src_ref=lesser.at[it, :, span(peer(j), c), :],
            dst_ref=band.at[it, 1, :, me, pl.ds(c * part, part), :],
            send_sem=a_send.at[it, c, j], recv_sem=a_recv.at[it, c, j],
            device_id={"momentum": peer(j)}, device_id_type=MESH)

    def halo(it, c, side):
        return pltpu.make_async_remote_copy(
            src_ref=band.at[it, 1, :, :, pl.ds(c * part, part), :],
            dst_ref=band.at[it, side, :, :, pl.ds(c * part, part), :],
            send_sem=h_send.at[it, c, side // 2], recv_sem=h_recv.at[it, c, side // 2],
            device_id={"energy": right if side == 0 else left}, device_id_type=MESH)

    def homeward(it, c, j):
        return pltpu.make_async_remote_copy(
            src_ref=mixed.at[it, peer(j), :, pl.ds(c * part, part), :],
            dst_ref=back.at[it, :, span(me, c), :],
            send_sem=b_send.at[it, c, j], recv_sem=b_recv.at[it, c, j],
            device_id={"momentum": peer(j)}, device_id_type=MESH)

    def mix(it, c):
        def step(n, carry):
            r = pl.ds(pl.multiple_of(c * part + n * PACK, PACK), PACK)

            def at(i, q):
                side, i = (0, i + energies) if i < 0 else (1, i) if i < energies else (2, i - energies)
                return band[it, side, i, q, r, :].astype(jnp.float32).reshape(2, PACK // 2, tile)

            for i in range(energies):
                pair = [[at(i - d, q) + at(i + d, q) for q in range(nk)] for d in range(1, OMAX + 1)]

                def one(k, inner):
                    total = None
                    for d in range(OMAX):
                        for q in range(nk):
                            term = weights[d, k, q][None] * pair[d][q]
                            total = term if total is None else total + term
                    mixed[it, k, i, r, :] = total.reshape(PACK, tile).astype(jnp.bfloat16)
                    return inner

                if nk <= 4:
                    for k in range(nk):
                        one(k, 0)
                else:
                    lax.fori_loop(0, nk, one, 0)
            return carry

        lax.fori_loop(0, part // PACK, step, 0)

    pl.semaphore_wait(barrier, nk - 1 + has_left.astype(jnp.int32) + has_right.astype(jnp.int32))
    loads[0].wait()
    source = start
    for it in range(ITERS):
        for i in range(energies):
            if it == 0:
                loads[1 + i].wait()
            onsite(it, i, source)
        for c in range(chunks):
            for j in range(1, nk):
                outward(it, c, j).start()
        mine = pltpu.make_async_copy(lesser.at[it, :, pl.ds(pl.multiple_of(me * rows, PACK), rows), :],
                                     band.at[it, 1, :, me], own_sem.at[it, chunks])
        mine.start()
        if it == ITERS - 1:
            store = pltpu.make_async_copy(lesser.at[it], lesser_out, out_sem.at[0])
            store.start()
        mine.wait()
        keeps = []
        for c in range(chunks + 1):
            if c < chunks:
                for j in range(1, nk):
                    outward(it, c, j).wait_recv()

                @pl.when(has_right)
                def _():
                    halo(it, c, 0).start()

                @pl.when(has_left)
                def _():
                    halo(it, c, 2).start()
            if c > 0:
                b = c - 1

                @pl.when(has_left)
                def _():
                    halo(it, b, 0).wait_recv()

                @pl.when(has_right)
                def _():
                    halo(it, b, 2).wait_recv()

                mix(it, b)
                for j in range(1, nk):
                    homeward(it, b, j).start()
                keep = pltpu.make_async_copy(mixed.at[it, me, :, pl.ds(b * part, part), :],
                                             back.at[it, :, span(me, b), :], own_sem.at[it, b])
                keep.start()
                keeps.append(keep)
        for c in range(chunks):
            keeps[c].wait()
            for j in range(1, nk):
                homeward(it, c, j).wait_recv()
        for i in range(energies):
            def add(n, carry):
                r = pl.ds(pl.multiple_of(n * tile, tile), tile)
                total = start[i, r, :].astype(jnp.float32) + back[it, i, r, :].astype(jnp.float32)
                sigma[it, i, r, :] = total.astype(jnp.bfloat16)
                return carry
            lax.fori_loop(0, 2 * tiles, add, 0)
        source = sigma.at[it]

    final = pltpu.make_async_copy(sigma.at[ITERS - 1], sigma_out, out_sem.at[1])
    final.start()
    for it in range(ITERS):
        for c in range(chunks):
            for j in range(1, nk):
                outward(it, c, j).wait_send()
                homeward(it, c, j).wait_send()

            @pl.when(has_right)
            def _():
                halo(it, c, 0).wait_send()

            @pl.when(has_left)
            def _():
                halo(it, c, 2).wait_send()
    store.wait()
    final.wait()


def body(ne, nk, green, contact, counts, offsets, pairs, table):
    energies, order = green.shape[0], green.shape[-1]
    tile = contact.shape[-1]
    height = contact.shape[2] * contact.shape[3] * tile
    rows = height // nk
    chunks = max(c for c in range(1, CHUNKS + 1) if rows % (c * PACK) == 0)
    blocks = green.reshape(energies, 2, order, order)
    flat = contact.reshape(energies, height, tile)
    half = jnp.bfloat16
    result = jax.ShapeDtypeStruct(flat.shape, half)
    dma = pltpu.SemaphoreType.DMA
    anywhere = pl.BlockSpec(memory_space=pl.ANY)
    scalars = pl.BlockSpec(memory_space=pltpu.SMEM)
    lesser, sigma = pl.pallas_call(
        functools.partial(born, ne, nk, chunks),
        out_shape=(result, result),
        in_specs=[anywhere] * 2 + [scalars] * 4,
        out_specs=(anywhere, anywhere),
        scratch_shapes=[
            pltpu.VMEM(blocks.shape, half),
            pltpu.VMEM(flat.shape, half),
            pltpu.VMEM((2, order, order), half),
            pltpu.VMEM((ITERS,) + flat.shape, half),
            pltpu.VMEM((ITERS, 3, energies, nk, rows, tile), half),
            pltpu.VMEM((ITERS, nk, energies, rows, tile), half),
            pltpu.VMEM((ITERS,) + flat.shape, half),
            pltpu.VMEM((ITERS,) + flat.shape, half),
            pltpu.VMEM((OMAX, nk, nk, 8, tile), jnp.float32),
            dma((energies + 1,)),
            dma((ITERS, chunks + 1)),
            dma((2,)),
            dma((ITERS, chunks, nk)),
            dma((ITERS, chunks, nk)),
            dma((ITERS, chunks, 2)),
            dma((ITERS, chunks, 2)),
            dma((ITERS, chunks, nk)),
            dma((ITERS, chunks, nk)),
        ],
        compiler_params=pltpu.CompilerParams(
            collective_id=0, has_side_effects=True, vmem_limit_bytes=40 * 2**20
        ),
    )(blocks, flat, counts, offsets, pairs, table)
    return lesser.reshape(contact.shape), sigma.reshape(contact.shape)


def solution(mesh):
    blocks = P("energy", "momentum", None, None, None)
    tiles = P("energy", "momentum", None, None, None, None)
    run = functools.partial(body, mesh.shape["energy"], mesh.shape["momentum"])
    return jax.shard_map(run, mesh=mesh, in_specs=(blocks, tiles, P("energy"), P(), P(), P()),
                         out_specs=(tiles, tiles), check_vma=False)
```

time: 213 us -> 54.7 us (0.26)
  the two profiles are of different devices: /device:TPU:9 before, /device:TPU:1 now
where the time goes in v1:
time: 54.7 us; the launch traced here: 54.2 us
  Pallas kernels  46.7 us (85%)
  local copies, waits for them, and re-layouts  6.85 us (13%)
  between operations  0.65 us (1%)
    pallas_call x1, Pallas kernels, body(): pl.pallas_call(functools.partial(born, ne, nk, chunks), out_shape=(result...  46.7 us
    unnamed x14, local copies, waits for them, and re-layouts  6.85 us

profile of v1, /device:TPU:1, one launch (start us, length us, event | category | flops | bytes accessed | tf_op | source)
XLA Modules:
  0.0 54.2 jit_solution(4824554281907393393)
XLA Ops:
  0.6 0.0 copy-start
  0.6 1.5 %copy-done = bf16[3,1,2,384,384]{4,3,2,1,0:T(8,128)(2,1)S(1)} copy-done((bf16[3,1,2,384,384]{4,3,2,1,0:T(8,128)(2,1)S(1)}, bf16[3,1,2,384,384]{4,3,2,1,0:T(8,128)(2,1)}, u32[]{:S(2)}) %copy-start) | copy-done | bytes 1769496
  2.1 0.0 copy-start.1
  2.1 1.1 %copy-done.1 = bf16[3,1,2,3,128,128]{5,4,3,2,1,0:T(8,128)(2,1)S(1)} copy-done((bf16[3,1,2,3,128,128]{5,4,3,2,1,0:T(8,128)(2,1)S(1)}, bf16[3,1,2,3,128,128]{5,4,3,2,1,0:T(8,128)(2,1)}, u32[]{:S(2)}) %copy-start.1) | copy-done | bytes 589848
  3.2 0.0 copy-start.2
  3.2 0.7 %copy-done.2 = s32[3,4,4]{2,1,0:T(4,128)S(1)} copy-done((s32[3,4,4]{2,1,0:T(4,128)S(1)}, s32[3,4,4]{2,1,0:T(4,128)}, u32[]{:S(2)}) %copy-start.2) | copy-done | bytes 216
  3.9 0.0 copy-start.3
  3.9 0.7 %copy-done.3 = f32[3,16]{1,0:T(4,128)S(1)} copy-done((f32[3,16]{1,0:T(4,128)S(1)}, f32[3,16]{1,0:T(4,128)}, u32[]{:S(2)}) %copy-start.3) | copy-done | bytes 216
  4.5 0.0 copy-start.4
  4.5 0.7 %copy-done.4 = s32[3]{0:T(128)S(1)} copy-done((s32[3]{0:T(128)S(1)}, s32[3]{0:T(128)}, u32[]{:S(2)}) %copy-start.4) | copy-done | bytes 36
  5.2 0.0 copy-start.5
  5.2 0.7 %copy-done.5 = s32[3]{0:T(128)S(1)} copy-done((s32[3]{0:T(128)S(1)}, s32[3]{0:T(128)}, u32[]{:S(2)}) %copy-start.5) | copy-done | bytes 36
  5.9 46.7 %shard_map.77 = (bf16[3,768,128]{2,1,0:T(8,128)(2,1)S(1)}, bf16[3,768,128]{2,1,0:T(8,128)(2,1)S(1)}) custom-call(bf16[3,2,384,384]{3,2,1,0:T(8,128)(2,1)S(1)} %bitcast.8, bf16[3,768,128]{2,1,0:T(8,128)(2,1)S(1)} %bitcast.11, s32[3]{0:T(128)S(1)} %copy-done.4, s32[3]{0:T(128)S(1)} %copy-done.5, s32[3,4,4]{2,1,0:T(4,128)S(1)} %copy-done.2, f32[3,16]{1,0:T(4,128)S(1)} %copy-done.3), custom_call_target="tpu_custom_call" | custom-call | tf_op jit(solution)/shard_map/pallas_call | solution.py:248
  52.5 0.8 %copy.12 = bf16[3,1,2,3,128,128]{5,4,3,2,1,0:T(8,128)(2,1)} copy(bf16[3,1,2,3,128,128]{5,4,3,2,1,0:T(8,128)(2,1)S(1)} %bitcast.10) | data formatting | bytes 1179648
  53.3 0.8 %copy.13 = bf16[3,1,2,3,128,128]{5,4,3,2,1,0:T(8,128)(2,1)} copy(bf16[3,1,2,3,128,128]{5,4,3,2,1,0:T(8,128)(2,1)S(1)} %bitcast.9) | data formatting | bytes 1179648
Async XLA Ops:
  0.6 1.5 %copy-start = (bf16[3,1,2,384,384]{4,3,2,1,0:T(8,128)(2,1)S(1)}, bf16[3,1,2,384,384]{4,3,2,1,0:T(8,128)(2,1)}, u32[]{:S(2)}) copy-start(bf16[3,1,2,384,384]{4,3,2,1,0:T(8,128)(2,1)} %param.6) | copy-start | bytes 5308420
  2.1 1.1 %copy-start.1 = (bf16[3,1,2,3,128,128]{5,4,3,2,1,0:T(8,128)(2,1)S(1)}, bf16[3,1,2,3,128,128]{5,4,3,2,1,0:T(8,128)(2,1)}, u32[]{:S(2)}) copy-start(bf16[3,1,2,3,128,128]{5,4,3,2,1,0:T(8,128)(2,1)} %param.7) | copy-start | bytes 1769476
  3.2 0.7 %copy-start.2 = (s32[3,4,4]{2,1,0:T(4,128)S(1)}, s32[3,4,4]{2,1,0:T(4,128)}, u32[]{:S(2)}) copy-start(s32[3,4,4]{2,1,0:T(4,128)} %pairs.1) | copy-start | bytes 580
  3.9 0.7 %copy-start.3 = (f32[3,16]{1,0:T(4,128)S(1)}, f32[3,16]{1,0:T(4,128)}, u32[]{:S(2)}) copy-start(f32[3,16]{1,0:T(4,128)} %table.1) | copy-start | bytes 580
  4.5 0.7 %copy-start.4 = (s32[3]{0:T(128)S(1)}, s32[3]{0:T(128)}, u32[]{:S(2)}) copy-start(s32[3]{0:T(128)} %counts.1) | copy-start | bytes 40
  5.2 0.7 %copy-start.5 = (s32[3]{0:T(128)S(1)}, s32[3]{0:T(128)}, u32[]{:S(2)}) copy-start(s32[3]{0:T(128)} %offsets.1) | copy-start | bytes 40

commit v2 on v1

--- a/solution.py
+++ b/solution.py
@@ -27,10 +27,16 @@
     has_left, has_right = e > 0, e < ne - 1
     left, right = jnp.maximum(e - 1, 0), jnp.minimum(e + 1, ne - 1)
 
-    loads = [pltpu.make_async_copy(contact, start, in_sem.at[energies])]
-    loads += [pltpu.make_async_copy(green.at[i], g.at[i], in_sem.at[i]) for i in range(energies)]
-    for load in loads:
-        load.start()
+    loads = []
+    for i in range(energies):
+        loads.append((pltpu.make_async_copy(contact.at[i], start.at[i], in_sem.at[0, i]),
+                      pltpu.make_async_copy(green.at[i], g.at[i], in_sem.at[1, i])))
+        for load in loads[i]:
+            load.start()
+
+    out_pieces = [(0, i, 1) for i in range(energies)] + [(c, 0, energies) for c in range(1, chunks)]
+    home_pieces = [(c, 0, energies) for c in range(chunks - 1)]
+    home_pieces += [(chunks - 1, i, 1) for i in range(energies)]
 
     def peer(j):
         return lax.rem(me + j, nk)
@@ -58,8 +64,6 @@
             weights[d, k, q] = jnp.full(weights.shape[3:], sums[d], jnp.float32)
         return carry
 
-    lax.fori_loop(0, nk * nk, weigh, 0)
-
     def clear(side):
         for it in range(ITERS):
             for i in range(energies):
@@ -68,13 +72,16 @@
                     return carry
                 lax.fori_loop(0, nk, zero, 0)
 
-    @pl.when(e == 0)
-    def _():
-        clear(0)
-
-    @pl.when(e == ne - 1)
-    def _():
-        clear(2)
+    def prepare():
+        lax.fori_loop(0, nk * nk, weigh, 0)
+
+        @pl.when(e == 0)
+        def _():
+            clear(0)
+
+        @pl.when(e == ne - 1)
+        def _():
+            clear(2)
 
     def onsite(it, i, source):
         for t in range(tiles):
@@ -101,11 +108,12 @@
     def span(owner, c):
         return pl.ds(pl.multiple_of(owner * rows + c * part, PACK), part)
 
-    def outward(it, c, j):
+    def outward(it, n, j):
+        c, i, w = out_pieces[n]
         return pltpu.make_async_remote_copy(
-            src_ref=lesser.at[it, :, span(peer(j), c), :],
-            dst_ref=band.at[it, 1, :, me, pl.ds(c * part, part), :],
-            send_sem=a_send.at[it, c, j], recv_sem=a_recv.at[it, c, j],
+            src_ref=lesser.at[it, pl.ds(i, w), span(peer(j), c), :],
+            dst_ref=band.at[it, 1, pl.ds(i, w), me, pl.ds(c * part, part), :],
+            send_sem=a_send.at[it, n, j], recv_sem=a_recv.at[it, n, j],
             device_id={"momentum": peer(j)}, device_id_type=MESH)
 
     def halo(it, c, side):
@@ -115,14 +123,20 @@
             send_sem=h_send.at[it, c, side // 2], recv_sem=h_recv.at[it, c, side // 2],
             device_id={"energy": right if side == 0 else left}, device_id_type=MESH)
 
-    def homeward(it, c, j):
+    def homeward(it, n, j):
+        c, i, w = home_pieces[n]
         return pltpu.make_async_remote_copy(
-            src_ref=mixed.at[it, peer(j), :, pl.ds(c * part, part), :],
-            dst_ref=back.at[it, :, span(me, c), :],
-            send_sem=b_send.at[it, c, j], recv_sem=b_recv.at[it, c, j],
+            src_ref=mixed.at[it, peer(j), pl.ds(i, w), pl.ds(c * part, part), :],
+            dst_ref=back.at[it, pl.ds(i, w), span(me, c), :],
+            send_sem=b_send.at[it, n, j], recv_sem=b_recv.at[it, n, j],
             device_id={"momentum": peer(j)}, device_id_type=MESH)
 
-    def mix(it, c):
+    def keep(it, n):
+        c, i, w = home_pieces[n]
+        return pltpu.make_async_copy(mixed.at[it, me, pl.ds(i, w), pl.ds(c * part, part), :],
+                                     back.at[it, pl.ds(i, w), span(me, c), :], own_sem.at[it, n])
+
+    def mix(it, c, first, width):
         def step(n, carry):
             r = pl.ds(pl.multiple_of(c * part + n * PACK, PACK), PACK)
 
@@ -130,7 +144,7 @@
                 side, i = (0, i + energies) if i < 0 else (1, i) if i < energies else (2, i - energies)
                 return band[it, side, i, q, r, :].astype(jnp.float32).reshape(2, PACK // 2, tile)
 
-            for i in range(energies):
+            for i in range(first, first + width):
                 pair = [[at(i - d, q) + at(i + d, q) for q in range(nk)] for d in range(1, OMAX + 1)]
 
                 def one(k, inner):
@@ -151,30 +165,56 @@
 
         lax.fori_loop(0, part // PACK, step, 0)
 
-    pl.semaphore_wait(barrier, nk - 1 + has_left.astype(jnp.int32) + has_right.astype(jnp.int32))
-    loads[0].wait()
+    def arrive(it, n):
+        keep(it, n).wait()
+        for j in range(1, nk):
+            homeward(it, n, j).wait_recv()
+
+    def renew(it, i):
+        if i == 0:
+            for n in range(chunks - 1):
+                arrive(it, n)
+        arrive(it, chunks - 1 + i)
+
+        def add(n, carry):
+            r = pl.ds(pl.multiple_of(n * tile, tile), tile)
+            total = start[i, r, :].astype(jnp.float32) + back[it, i, r, :].astype(jnp.float32)
+            sigma[it, i, r, :] = total.astype(jnp.bfloat16)
+            return carry
+        lax.fori_loop(0, 2 * tiles, add, 0)
+
     source = start
     for it in range(ITERS):
         for i in range(energies):
             if it == 0:
-                loads[1 + i].wait()
+                for load in loads[i]:
+                    load.wait()
+            else:
+                renew(it - 1, i)
             onsite(it, i, source)
-        for c in range(chunks):
+            if it == 0 and i == 0:
+                pl.semaphore_wait(
+                    barrier, nk - 1 + has_left.astype(jnp.int32) + has_right.astype(jnp.int32))
             for j in range(1, nk):
-                outward(it, c, j).start()
+                outward(it, i, j).start()
+        for n in range(energies, len(out_pieces)):
+            for j in range(1, nk):
+                outward(it, n, j).start()
         mine = pltpu.make_async_copy(lesser.at[it, :, pl.ds(pl.multiple_of(me * rows, PACK), rows), :],
-                                     band.at[it, 1, :, me], own_sem.at[it, chunks])
+                                     band.at[it, 1, :, me], own_sem.at[it, len(home_pieces)])
         mine.start()
         if it == ITERS - 1:
-            store = pltpu.make_async_copy(lesser.at[it], lesser_out, out_sem.at[0])
+            store = pltpu.make_async_copy(lesser.at[it], lesser_out, out_sem.at[energies])
             store.start()
+        if it == 0:
+            prepare()
         mine.wait()
-        keeps = []
         for c in range(chunks + 1):
+            for n, (piece, _, _) in enumerate(out_pieces):
+                if piece == c:
+                    for j in range(1, nk):
+                        outward(it, n, j).wait_recv()
             if c < chunks:
-                for j in range(1, nk):
-                    outward(it, c, j).wait_recv()
-
                 @pl.when(has_right)
                 def _():
                     halo(it, c, 0).start()
@@ -183,44 +223,34 @@
                 def _():
                     halo(it, c, 2).start()
             if c > 0:
-                b = c - 1
-
                 @pl.when(has_left)
                 def _():
-                    halo(it, b, 0).wait_recv()
+                    halo(it, c - 1, 0).wait_recv()
 
                 @pl.when(has_right)
                 def _():
-                    halo(it, b, 2).wait_recv()
-
-                mix(it, b)
-                for j in range(1, nk):
-                    homeward(it, b, j).start()
-                keep = pltpu.make_async_copy(mixed.at[it, me, :, pl.ds(b * part, part), :],
-                                             back.at[it, :, span(me, b), :], own_sem.at[it, b])
-                keep.start()
-                keeps.append(keep)
+                    halo(it, c - 1, 2).wait_recv()
+
+                for n, (piece, first, width) in enumerate(home_pieces):
+                    if piece == c - 1:
+                        mix(it, piece, first, width)
+                        for j in range(1, nk):
+                            homeward(it, n, j).start()
+                        keep(it, n).start()
+        source = sigma.at[it]
+
+    last = ITERS - 1
+    final = [pltpu.make_async_copy(sigma.at[last, i], sigma_out.at[i], out_sem.at[i])
+             for i in range(energies)]
+    for i in range(energies):
+        renew(last, i)
+        final[i].start()
+    for it in range(ITERS):
+        for n in range(len(out_pieces)):
+            for j in range(1, nk):
+                outward(it, n, j).wait_send()
+                homeward(it, n, j).wait_send()
         for c in range(chunks):
-            keeps[c].wait()
-            for j in range(1, nk):
-                homeward(it, c, j).wait_recv()
-        for i in range(energies):
-            def add(n, carry):
-                r = pl.ds(pl.multiple_of(n * tile, tile), tile)
-                total = start[i, r, :].astype(jnp.float32) + back[it, i, r, :].astype(jnp.float32)
-                sigma[it, i, r, :] = total.astype(jnp.bfloat16)
-                return carry
-            lax.fori_loop(0, 2 * tiles, add, 0)
-        source = sigma.at[it]
-
-    final = pltpu.make_async_copy(sigma.at[ITERS - 1], sigma_out, out_sem.at[1])
-    final.start()
-    for it in range(ITERS):
-        for c in range(chunks):
-            for j in range(1, nk):
-                outward(it, c, j).wait_send()
-                homeward(it, c, j).wait_send()
-
             @pl.when(has_right)
             def _():
                 halo(it, c, 0).wait_send()
@@ -229,7 +259,8 @@
             def _():
                 halo(it, c, 2).wait_send()
     store.wait()
-    final.wait()
+    for i in range(energies):
+        final[i].wait()
 
 
 def body(ne, nk, green, contact, counts, offsets, pairs, table):
@@ -238,6 +269,7 @@
     height = contact.shape[2] * contact.shape[3] * tile
     rows = height // nk
     chunks = max(c for c in range(1, CHUNKS + 1) if rows % (c * PACK) == 0)
+    pieces = energies + chunks - 1
     blocks = green.reshape(energies, 2, order, order)
     flat = contact.reshape(energies, height, tile)
     half = jnp.bfloat16
@@ -260,18 +292,18 @@
             pltpu.VMEM((ITERS,) + flat.shape, half),
             pltpu.VMEM((ITERS,) + flat.shape, half),
             pltpu.VMEM((OMAX, nk, nk, 8, tile), jnp.float32),
+            dma((2, energies)),
+            dma((ITERS, pieces + 1)),
             dma((energies + 1,)),
-            dma((ITERS, chunks + 1)),
-            dma((2,)),
-            dma((ITERS, chunks, nk)),
-            dma((ITERS, chunks, nk)),
+            dma((ITERS, pieces, nk)),
+            dma((ITERS, pieces, nk)),
             dma((ITERS, chunks, 2)),
             dma((ITERS, chunks, 2)),
-            dma((ITERS, chunks, nk)),
-            dma((ITERS, chunks, nk)),
+            dma((ITERS, pieces, nk)),
+            dma((ITERS, pieces, nk)),
         ],
         compiler_params=pltpu.CompilerParams(
-            collective_id=0, has_side_effects=True, vmem_limit_bytes=40 * 2**20
+            collective_id=0, has_side_effects=True, vmem_limit_bytes=60 * 2**20
         ),
     )(blocks, flat, counts, offsets, pairs, table)
     return lesser.reshape(contact.shape), sigma.reshape(contact.shape)

time: 54.7 us -> 48.3 us (0.88)
  Pallas kernels: 46.7 us -> 43.6 us
  local copies, waits for them, and re-layouts: 6.85 us -> 3.86 us
    pallas_call x1, Pallas kernels: 46.7 us -> 43.6 us  [body(): pl.pallas_call(functools.partial(born, ne, nk, chunks), out_shape=(result...]
    unnamed x14 -> x2, local copies, waits for them, and re-layouts: 6.85 us -> 3.86 us
where the time goes in v2:
time: 48.3 us; the launch traced here: 48.1 us
  Pallas kernels  43.6 us (90%)
  local copies, waits for them, and re-layouts  3.86 us (8%)
  between operations  0.64 us (1%)
    pallas_call x1, Pallas kernels, body(): pl.pallas_call(functools.partial(born, ne, nk, chunks), out_shape=(result...  43.6 us
    unnamed x2, local copies, waits for them, and re-layouts  3.86 us

profile of v2, /device:TPU:1, one launch (start us, length us, event | category | flops | bytes accessed | tf_op | source)
XLA Modules:
  0.0 48.1 jit_solution(11217550670961692297)
XLA Ops:
  0.6 43.6 %shard_map.77 = (bf16[3,768,128]{2,1,0:T(8,128)(2,1)}, bf16[3,768,128]{2,1,0:T(8,128)(2,1)}) custom-call(bf16[3,2,384,384]{3,2,1,0:T(8,128)(2,1)} %bitcast.8, bf16[3,768,128]{2,1,0:T(8,128)(2,1)} %bitcast.11, s32[3]{0:T(128)} %counts.1, s32[3]{0:T(128)} %offsets.1, s32[3,4,4]{2,1,0:T(4,128)} %pairs.1, f32[3,16]{1,0:T(4,128)} %table.1), custom_call_target="tpu_custom_call" | custom-call | tf_op jit(solution)/shard_map/pallas_call | solution.py:280
  44.2 1.9 %copy.12 = bf16[3,1,2,3,128,128]{5,4,3,2,1,0:T(8,128)(2,1)} copy(bf16[3,1,2,3,128,128]{5,4,3,2,1,0:T(8,128)(2,1)} %bitcast.10) | data formatting | bytes 1179648
  46.1 1.9 %copy.13 = bf16[3,1,2,3,128,128]{5,4,3,2,1,0:T(8,128)(2,1)} copy(bf16[3,1,2,3,128,128]{5,4,3,2,1,0:T(8,128)(2,1)} %bitcast.9) | data formatting | bytes 1179648

commit v3 on v2

--- a/solution.py
+++ b/solution.py
@@ -10,7 +10,7 @@
 OMAX = 3
 ITERS = 2
 PACK = 16
-CHUNKS = 3
+CHUNKS = 4
 MESH = pl.DeviceIdType.MESH
 
 
@@ -170,7 +170,7 @@
         for j in range(1, nk):
             homeward(it, n, j).wait_recv()
 
-    def renew(it, i):
+    def renew(it, i, result):
         if i == 0:
             for n in range(chunks - 1):
                 arrive(it, n)
@@ -179,7 +179,7 @@
         def add(n, carry):
             r = pl.ds(pl.multiple_of(n * tile, tile), tile)
             total = start[i, r, :].astype(jnp.float32) + back[it, i, r, :].astype(jnp.float32)
-            sigma[it, i, r, :] = total.astype(jnp.bfloat16)
+            result[i, r, :] = total.astype(jnp.bfloat16)
             return carry
         lax.fori_loop(0, 2 * tiles, add, 0)
 
@@ -190,7 +190,7 @@
                 for load in loads[i]:
                     load.wait()
             else:
-                renew(it - 1, i)
+                renew(it - 1, i, source)
             onsite(it, i, source)
             if it == 0 and i == 0:
                 pl.semaphore_wait(
@@ -204,7 +204,7 @@
                                      band.at[it, 1, :, me], own_sem.at[it, len(home_pieces)])
         mine.start()
         if it == ITERS - 1:
-            store = pltpu.make_async_copy(lesser.at[it], lesser_out, out_sem.at[energies])
+            store = pltpu.make_async_copy(lesser.at[it], lesser_out, out_sem.at[0])
             store.start()
         if it == 0:
             prepare()
@@ -237,14 +237,10 @@
                         for j in range(1, nk):
                             homeward(it, n, j).start()
                         keep(it, n).start()
-        source = sigma.at[it]
-
-    last = ITERS - 1
-    final = [pltpu.make_async_copy(sigma.at[last, i], sigma_out.at[i], out_sem.at[i])
-             for i in range(energies)]
+        source = sigma.at[it] if it < ITERS - 1 else sigma_out
+
     for i in range(energies):
-        renew(last, i)
-        final[i].start()
+        renew(ITERS - 1, i, source)
     for it in range(ITERS):
         for n in range(len(out_pieces)):
             for j in range(1, nk):
@@ -259,8 +255,15 @@
             def _():
                 halo(it, c, 2).wait_send()
     store.wait()
-    for i in range(energies):
-        final[i].wait()
+
+
+def write(*refs):
+    count = (len(refs) - 1) // 2
+    copies = [pltpu.make_async_copy(refs[i], refs[count + i], refs[-1].at[i]) for i in range(count)]
+    for copy in copies:
+        copy.start()
+    for copy in copies:
+        copy.wait()
 
 
 def body(ne, nk, green, contact, counts, offsets, pairs, table):
@@ -276,12 +279,14 @@
     result = jax.ShapeDtypeStruct(flat.shape, half)
     dma = pltpu.SemaphoreType.DMA
     anywhere = pl.BlockSpec(memory_space=pl.ANY)
+    far = pl.BlockSpec(memory_space=pltpu.HBM)
+    near = pl.BlockSpec(memory_space=pltpu.VMEM)
     scalars = pl.BlockSpec(memory_space=pltpu.SMEM)
-    lesser, sigma = pl.pallas_call(
+    results = pl.pallas_call(
         functools.partial(born, ne, nk, chunks),
-        out_shape=(result, result),
-        in_specs=[anywhere] * 2 + [scalars] * 4,
-        out_specs=(anywhere, anywhere),
+        out_shape=(pltpu.VMEM(flat.shape, half),) * 2,
+        in_specs=[far] * 2 + [scalars] * 4,
+        out_specs=(near, near),
         scratch_shapes=[
             pltpu.VMEM(blocks.shape, half),
             pltpu.VMEM(flat.shape, half),
@@ -290,11 +295,11 @@
             pltpu.VMEM((ITERS, 3, energies, nk, rows, tile), half),
             pltpu.VMEM((ITERS, nk, energies, rows, tile), half),
             pltpu.VMEM((ITERS,) + flat.shape, half),
-            pltpu.VMEM((ITERS,) + flat.shape, half),
+            pltpu.VMEM((ITERS - 1,) + flat.shape, half),
             pltpu.VMEM((OMAX, nk, nk, 8, tile), jnp.float32),
             dma((2, energies)),
             dma((ITERS, pieces + 1)),
-            dma((energies + 1,)),
+            dma((1,)),
             dma((ITERS, pieces, nk)),
             dma((ITERS, pieces, nk)),
             dma((ITERS, chunks, 2)),
@@ -303,9 +308,16 @@
             dma((ITERS, pieces, nk)),
         ],
         compiler_params=pltpu.CompilerParams(
-            collective_id=0, has_side_effects=True, vmem_limit_bytes=60 * 2**20
+            collective_id=0, has_side_effects=True, vmem_limit_bytes=56 * 2**20
         ),
     )(blocks, flat, counts, offsets, pairs, table)
+    lesser, sigma = pl.pallas_call(
+        write,
+        out_shape=(result, result),
+        in_specs=[anywhere] * 2,
+        out_specs=(far, far),
+        scratch_shapes=[dma((2,))],
+    )(*results)
     return lesser.reshape(contact.shape), sigma.reshape(contact.shape)
 
 

time: 48.3 us -> 82.5 us (1.71)
  Pallas kernels: 43.6 us -> 79.8 us
  local copies, waits for them, and re-layouts: 3.86 us -> 1.63 us
    pallas_call x1 -> x2, Pallas kernels: 43.6 us -> 79.8 us  [the longest x1 42.9 us: body(): pl.pallas_call(functools.partial(born, ne, nk, chunks), out_shape=(pltpu....]
    unnamed x2 -> x4, local copies, waits for them, and re-layouts: 3.86 us -> 1.63 us
where the time goes in v3:
time: 82.5 us; the launch traced here: 82 us
  Pallas kernels  79.8 us (97%)
  local copies, waits for them, and re-layouts  1.63 us (2%)
    pallas_call x1, Pallas kernels, body(): pl.pallas_call(functools.partial(born, ne, nk, chunks), out_shape=(pltpu....  42.9 us
    pallas_call x1, Pallas kernels, body(): pl.pallas_call(write, out_shape=(result, result), in_specs=[anywhere] * 2...  36.9 us

profile of v3, /device:TPU:1, one launch (start us, length us, event | category | flops | bytes accessed | tf_op | source)
XLA Modules:
  0.0 82.0 jit_solution(4248746661896943425)
XLA Ops:
  0.6 42.9 %shard_map.77 = (bf16[3,768,128]{2,1,0:T(8,128)(2,1)S(1)}, bf16[3,768,128]{2,1,0:T(8,128)(2,1)S(1)}) custom-call(bf16[3,2,384,384]{3,2,1,0:T(8,128)(2,1)} %bitcast.8, bf16[3,768,128]{2,1,0:T(8,128)(2,1)} %bitcast.9, s32[3]{0:T(128)} %counts.1, s32[3]{0:T(128)} %offsets.1, s32[3,4,4]{2,1,0:T(4,128)} %pairs.1, f32[3,16]{1,0:T(4,128)} %table.1), custom_call_target="tpu_custom_call" | custom-call | tf_op jit(solution)/shard_map/pallas_call | solution.py:285
  43.6 0.0 copy-start
  43.6 0.8 copy-done
  44.4 0.0 copy-start.1
  44.4 0.8 copy-done.1
  45.2 36.9 %shard_map.78 = (bf16[3,768,128]{2,1,0:T(8,128)(2,1)}, bf16[3,768,128]{2,1,0:T(8,128)(2,1)}) custom-call(bf16[3,768,128]{2,1,0:T(8,128)(2,1)} %copy-done, bf16[3,768,128]{2,1,0:T(8,128)(2,1)} %copy-done.1), custom_call_target="tpu_custom_call" | custom-call | tf_op jit(solution)/shard_map/pallas_call | solution.py:314
Async XLA Ops:
  43.6 0.8 copy-start
  44.4 0.8 copy-start.1

commit v4 on v3

--- a/solution.py
+++ b/solution.py
@@ -10,17 +10,17 @@
 OMAX = 3
 ITERS = 2
 PACK = 16
-CHUNKS = 4
 MESH = pl.DeviceIdType.MESH
 
 
-def born(ne, nk, chunks, green, contact, counts, offsets, pairs, table, lesser_out, sigma_out,
+def born(ne, nk, green, contact, counts, offsets, pairs, table, lesser_out, sigma_out,
          g, start, product, lesser, band, mixed, back, sigma, weights,
-         in_sem, own_sem, out_sem, a_send, a_recv, h_send, h_recv, b_send, b_recv):
+         in_sem, own_sem, a_send, a_recv, h_send, h_recv, b_send, b_recv):
     energies, order = g.shape[0], g.shape[-1]
     tile = start.shape[-1]
     tiles = order // tile
     rows = band.shape[4]
+    chunks = tiles
     part = rows // chunks
     modes = offsets.shape[0]
     e, me = lax.axis_index("energy"), lax.axis_index("momentum")
@@ -83,30 +83,32 @@
         def _():
             clear(2)
 
-    def onsite(it, i, source):
-        for t in range(tiles):
-            cols = slice(t * tile, (t + 1) * tile)
-            s_real = source[i, t * tile:(t + 1) * tile, :]
-            s_imag = source[i, (tiles + t) * tile:(tiles + t + 1) * tile, :]
-            s = jnp.concatenate([jnp.concatenate([s_real, s_imag], 1),
-                                 jnp.concatenate([-s_imag, s_real], 1)], 0)
-            a = jnp.concatenate([g[i, 0, :, cols], g[i, 1, :, cols]], 1)
-            p = jnp.dot(a, s, preferred_element_type=jnp.float32).astype(jnp.bfloat16)
-            product[0, :, cols] = p[:, :tile]
-            product[1, :, cols] = p[:, tile:]
-        for t in range(tiles):
-            r = slice(t * tile, (t + 1) * tile)
-            p = jnp.concatenate([product[0, r, :], product[1, r, :]], 0)
-            h = jnp.concatenate([g[i, 0, r, :], g[i, 1, r, :]], 0)
-            o = lax.dot_general(p, h, (((1,), (1,)), ((), ())), preferred_element_type=jnp.float32)
-            live = jnp.where(t < counts[i], jnp.float32(1), jnp.float32(0))
-            real = (o[:tile, :tile] + o[tile:, tile:]) * live
-            imag = (o[tile:, :tile] - o[:tile, tile:]) * live
-            lesser[it, i, t * tile:(t + 1) * tile, :] = real.astype(jnp.bfloat16)
-            lesser[it, i, (tiles + t) * tile:(tiles + t + 1) * tile, :] = imag.astype(jnp.bfloat16)
+    def project(i, t, source):
+        cols = slice(t * tile, (t + 1) * tile)
+        s_real, s_imag = source[i, 0, t], source[i, 1, t]
+        s = jnp.concatenate([jnp.concatenate([s_real, s_imag], 1),
+                             jnp.concatenate([-s_imag, s_real], 1)], 0)
+        a = jnp.concatenate([g[i, 0, :, cols], g[i, 1, :, cols]], 1)
+        p = jnp.dot(a, s, preferred_element_type=jnp.float32).astype(jnp.bfloat16)
+        product[i, 0, :, cols] = p[:, :tile]
+        product[i, 1, :, cols] = p[:, tile:]
+
+    def onsite(it, i, t):
+        r = slice(t * tile, (t + 1) * tile)
+        p = jnp.concatenate([product[i, 0, r, :], product[i, 1, r, :]], 0)
+        h = jnp.concatenate([g[i, 0, r, :], g[i, 1, r, :]], 0)
+        o = lax.dot_general(p, h, (((1,), (1,)), ((), ())), preferred_element_type=jnp.float32)
+        live = jnp.where(t < counts[i], jnp.float32(1), jnp.float32(0))
+        real = ((o[:tile, :tile] + o[tile:, tile:]) * live).astype(jnp.bfloat16)
+        imag = ((o[tile:, :tile] - o[:tile, tile:]) * live).astype(jnp.bfloat16)
+        lesser[it, i, 2 * t * tile:(2 * t + 1) * tile, :] = real
+        lesser[it, i, (2 * t + 1) * tile:(2 * t + 2) * tile, :] = imag
+        if it == ITERS - 1:
+            lesser_out[i, 0, t] = real
+            lesser_out[i, 1, t] = imag
 
     def span(owner, c):
-        return pl.ds(pl.multiple_of(owner * rows + c * part, PACK), part)
+        return pl.ds(pl.multiple_of(c * 2 * tile + owner * part, PACK), part)
 
     def outward(it, n, j):
         c, i, w = out_pieces[n]
@@ -116,6 +118,17 @@
             send_sem=a_send.at[it, n, j], recv_sem=a_recv.at[it, n, j],
             device_id={"momentum": peer(j)}, device_id_type=MESH)
 
+    def mine(it, n):
+        c, i, w = out_pieces[n]
+        return pltpu.make_async_copy(lesser.at[it, pl.ds(i, w), span(me, c), :],
+                                     band.at[it, 1, pl.ds(i, w), me, pl.ds(c * part, part), :],
+                                     own_sem.at[it, 0, n])
+
+    def send(it, n):
+        for j in range(1, nk):
+            outward(it, n, j).start()
+        mine(it, n).start()
+
     def halo(it, c, side):
         return pltpu.make_async_remote_copy(
             src_ref=band.at[it, 1, :, :, pl.ds(c * part, part), :],
@@ -134,7 +147,7 @@
     def keep(it, n):
         c, i, w = home_pieces[n]
         return pltpu.make_async_copy(mixed.at[it, me, pl.ds(i, w), pl.ds(c * part, part), :],
-                                     back.at[it, pl.ds(i, w), span(me, c), :], own_sem.at[it, n])
+                                     back.at[it, pl.ds(i, w), span(me, c), :], own_sem.at[it, 1, n])
 
     def mix(it, c, first, width):
         def step(n, carry):
@@ -170,48 +183,44 @@
         for j in range(1, nk):
             homeward(it, n, j).wait_recv()
 
-    def renew(it, i, result):
-        if i == 0:
-            for n in range(chunks - 1):
-                arrive(it, n)
-        arrive(it, chunks - 1 + i)
-
-        def add(n, carry):
-            r = pl.ds(pl.multiple_of(n * tile, tile), tile)
-            total = start[i, r, :].astype(jnp.float32) + back[it, i, r, :].astype(jnp.float32)
-            result[i, r, :] = total.astype(jnp.bfloat16)
-            return carry
-        lax.fori_loop(0, 2 * tiles, add, 0)
-
-    source = start
+    def renew(it, i, t, result):
+        for x in range(2):
+            r = slice((2 * t + x) * tile, (2 * t + x + 1) * tile)
+            total = start[i, x, t].astype(jnp.float32) + back[it, i, r, :].astype(jnp.float32)
+            result[i, x, t] = total.astype(jnp.bfloat16)
+
     for it in range(ITERS):
-        for i in range(energies):
-            if it == 0:
+        if it == 0:
+            for i in range(energies):
                 for load in loads[i]:
                     load.wait()
-            else:
-                renew(it - 1, i, source)
-            onsite(it, i, source)
-            if it == 0 and i == 0:
-                pl.semaphore_wait(
-                    barrier, nk - 1 + has_left.astype(jnp.int32) + has_right.astype(jnp.int32))
-            for j in range(1, nk):
-                outward(it, i, j).start()
+                for t in range(tiles):
+                    project(i, t, start)
+                onsite(it, i, 0)
+                if i == 0:
+                    pl.semaphore_wait(
+                        barrier, nk - 1 + has_left.astype(jnp.int32) + has_right.astype(jnp.int32))
+                send(it, i)
+        else:
+            for n, (t, first, width) in enumerate(home_pieces):
+                arrive(it - 1, n)
+                for i in range(first, first + width):
+                    renew(it - 1, i, t, sigma.at[it - 1])
+                    project(i, t, sigma.at[it - 1])
+            for i in range(energies):
+                onsite(it, i, 0)
+                send(it, i)
         for n in range(energies, len(out_pieces)):
-            for j in range(1, nk):
-                outward(it, n, j).start()
-        mine = pltpu.make_async_copy(lesser.at[it, :, pl.ds(pl.multiple_of(me * rows, PACK), rows), :],
-                                     band.at[it, 1, :, me], own_sem.at[it, len(home_pieces)])
-        mine.start()
-        if it == ITERS - 1:
-            store = pltpu.make_async_copy(lesser.at[it], lesser_out, out_sem.at[0])
-            store.start()
+            t = out_pieces[n][0]
+            for i in range(energies):
+                onsite(it, i, t)
+            send(it, n)
         if it == 0:
             prepare()
-        mine.wait()
         for c in range(chunks + 1):
             for n, (piece, _, _) in enumerate(out_pieces):
                 if piece == c:
+                    mine(it, n).wait()
                     for j in range(1, nk):
                         outward(it, n, j).wait_recv()
             if c < chunks:
@@ -237,10 +246,11 @@
                         for j in range(1, nk):
                             homeward(it, n, j).start()
                         keep(it, n).start()
-        source = sigma.at[it] if it < ITERS - 1 else sigma_out
-
-    for i in range(energies):
-        renew(ITERS - 1, i, source)
+
+    for n, (t, first, width) in enumerate(home_pieces):
+        arrive(ITERS - 1, n)
+        for i in range(first, first + width):
+            renew(ITERS - 1, i, t, sigma_out)
     for it in range(ITERS):
         for n in range(len(out_pieces)):
             for j in range(1, nk):
@@ -254,7 +264,6 @@
             @pl.when(has_left)
             def _():
                 halo(it, c, 2).wait_send()
-    store.wait()
 
 
 def write(*refs):
@@ -271,35 +280,35 @@
     tile = contact.shape[-1]
     height = contact.shape[2] * contact.shape[3] * tile
     rows = height // nk
-    chunks = max(c for c in range(1, CHUNKS + 1) if rows % (c * PACK) == 0)
+    chunks = contact.shape[3]
     pieces = energies + chunks - 1
     blocks = green.reshape(energies, 2, order, order)
-    flat = contact.reshape(energies, height, tile)
+    parted = contact.reshape((energies,) + contact.shape[2:])
+    flat = jax.ShapeDtypeStruct((energies, height, tile), contact.dtype)
     half = jnp.bfloat16
-    result = jax.ShapeDtypeStruct(flat.shape, half)
+    result = jax.ShapeDtypeStruct(parted.shape, half)
     dma = pltpu.SemaphoreType.DMA
     anywhere = pl.BlockSpec(memory_space=pl.ANY)
     far = pl.BlockSpec(memory_space=pltpu.HBM)
     near = pl.BlockSpec(memory_space=pltpu.VMEM)
     scalars = pl.BlockSpec(memory_space=pltpu.SMEM)
     results = pl.pallas_call(
-        functools.partial(born, ne, nk, chunks),
-        out_shape=(pltpu.VMEM(flat.shape, half),) * 2,
+        functools.partial(born, ne, nk),
+        out_shape=(pltpu.VMEM(parted.shape, half),) * 2,
         in_specs=[far] * 2 + [scalars] * 4,
         out_specs=(near, near),
         scratch_shapes=[
             pltpu.VMEM(blocks.shape, half),
-            pltpu.VMEM(flat.shape, half),
-            pltpu.VMEM((2, order, order), half),
+            pltpu.VMEM(parted.shape, half),
+            pltpu.VMEM(blocks.shape, half),
             pltpu.VMEM((ITERS,) + flat.shape, half),
             pltpu.VMEM((ITERS, 3, energies, nk, rows, tile), half),
             pltpu.VMEM((ITERS, nk, energies, rows, tile), half),
             pltpu.VMEM((ITERS,) + flat.shape, half),
-            pltpu.VMEM((ITERS - 1,) + flat.shape, half),
+            pltpu.VMEM((ITERS - 1,) + parted.shape, half),
             pltpu.VMEM((OMAX, nk, nk, 8, tile), jnp.float32),
             dma((2, energies)),
-            dma((ITERS, pieces + 1)),
-            dma((1,)),
+            dma((ITERS, 2, pieces)),
             dma((ITERS, pieces, nk)),
             dma((ITERS, pieces, nk)),
             dma((ITERS, chunks, 2)),
@@ -310,13 +319,14 @@
         compiler_params=pltpu.CompilerParams(
             collective_id=0, has_side_effects=True, vmem_limit_bytes=56 * 2**20
         ),
-    )(blocks, flat, counts, offsets, pairs, table)
+    )(blocks, parted, counts, offsets, pairs, table)
     lesser, sigma = pl.pallas_call(
         write,
         out_shape=(result, result),
-        in_specs=[anywhere] * 2,
-        out_specs=(far, far),
+        in_specs=[near] * 2,
+        out_specs=(anywhere, anywhere),
         scratch_shapes=[dma((2,))],
+        compiler_params=pltpu.CompilerParams(vmem_limit_bytes=4 * 2**20),
     )(*results)
     return lesser.reshape(contact.shape), sigma.reshape(contact.shape)
 

time: 82.5 us -> 45.5 us (0.55)
  Pallas kernels: 79.8 us -> 44.7 us
  local copies, waits for them, and re-layouts: 1.63 us -> 0 us
    pallas_call x2, Pallas kernels: 79.8 us -> 44.7 us  [the longest x1 43.7 us: body(): pl.pallas_call(functools.partial(born, ne, nk), out_shape=(pltpu.VMEM(par...]
    unnamed x4 -> x0, local copies, waits for them, and re-layouts: 1.63 us -> none
where the time goes in v4:
time: 45.5 us; the launch traced here: 45.3 us
  Pallas kernels  44.7 us (98%)
  between operations  0.64 us (1%)
    pallas_call x1, Pallas kernels, body(): pl.pallas_call(functools.partial(born, ne, nk), out_shape=(pltpu.VMEM(par...  43.7 us
    pallas_call x1, Pallas kernels, body(): pl.pallas_call(write, out_shape=(result, result), in_specs=[near] * 2, ou...  1.03 us

profile of v4, /device:TPU:1, one launch (start us, length us, event | category | flops | bytes accessed | tf_op | source)
XLA Modules:
  0.0 45.3 jit_solution(7757638819481729130)
XLA Ops:
  0.6 43.7 %shard_map.77 = (bf16[3,2,3,128,128]{4,3,2,1,0:T(8,128)(2,1)S(1)}, bf16[3,2,3,128,128]{4,3,2,1,0:T(8,128)(2,1)S(1)}) custom-call(bf16[3,2,384,384]{3,2,1,0:T(8,128)(2,1)} %bitcast.8, bf16[3,2,3,128,128]{4,3,2,1,0:T(8,128)(2,1)} %bitcast.9, s32[3]{0:T(128)} %counts.1, s32[3]{0:T(128)} %offsets.1, s32[3,4,4]{2,1,0:T(4,128)} %pairs.1, f32[3,16]{1,0:T(4,128)} %table.1), custom_call_target="tpu_custom_call" | custom-call | tf_op jit(solution)/shard_map/pallas_call | solution.py:295
  44.3 1.0 %shard_map.78 = (bf16[3,2,3,128,128]{4,3,2,1,0:T(8,128)(2,1)}, bf16[3,2,3,128,128]{4,3,2,1,0:T(8,128)(2,1)}) custom-call(bf16[3,2,3,128,128]{4,3,2,1,0:T(8,128)(2,1)S(1)} %get-tuple-element.6.refs_0_, bf16[3,2,3,128,128]{4,3,2,1,0:T(8,128)(2,1)S(1)} %get-tuple-element.7.refs_1_), custom_call_target="tpu_custom_call" | custom-call | tf_op jit(solution)/shard_map/pallas_call | solution.py:323

commit v5 on v4

--- a/solution.py
+++ b/solution.py
@@ -1,4 +1,5 @@
 import functools
+import math
 
 import jax
 import jax.numpy as jnp
@@ -24,8 +25,9 @@
     part = rows // chunks
     modes = offsets.shape[0]
     e, me = lax.axis_index("energy"), lax.axis_index("momentum")
-    has_left, has_right = e > 0, e < ne - 1
-    left, right = jnp.maximum(e - 1, 0), jnp.minimum(e + 1, ne - 1)
+    odd = lax.rem(e, 2)
+    near, far = e + 1 - 2 * odd, e - 1 + 2 * odd
+    has_near, has_far = near < ne, (far >= 0) & (far < ne)
 
     loads = []
     for i in range(energies):
@@ -38,20 +40,26 @@
     home_pieces = [(c, 0, energies) for c in range(chunks - 1)]
     home_pieces += [(chunks - 1, i, 1) for i in range(energies)]
 
+    side = math.isqrt(nk)
+
     def peer(j):
-        return lax.rem(me + j, nk)
+        if side * side != nk:
+            return lax.rem(me + j, nk)
+        high, low = j // side, j % side
+        high, low = high + odd * (low - high), low + odd * (high - low)
+        return lax.rem(me // side + high, side) * side + lax.rem(me % side + low, side)
 
     barrier = pltpu.get_barrier_semaphore()
     for j in range(1, nk):
         pl.semaphore_signal(barrier, inc=1, device_id={"momentum": peer(j)}, device_id_type=MESH)
 
-    @pl.when(has_left)
+    @pl.when(has_near)
     def _():
-        pl.semaphore_signal(barrier, inc=1, device_id={"energy": left}, device_id_type=MESH)
-
-    @pl.when(has_right)
+        pl.semaphore_signal(barrier, inc=1, device_id={"energy": near}, device_id_type=MESH)
+
+    @pl.when(has_far)
     def _():
-        pl.semaphore_signal(barrier, inc=1, device_id={"energy": right}, device_id_type=MESH)
+        pl.semaphore_signal(barrier, inc=1, device_id={"energy": far}, device_id_type=MESH)
 
     def weigh(i, carry):
         k, q = i // nk, i % nk
@@ -127,14 +135,15 @@
     def send(it, n):
         for j in range(1, nk):
             outward(it, n, j).start()
-        mine(it, n).start()
-
-    def halo(it, c, side):
+        mine(it, n).start(priority=1)
+
+    def halo(it, c, step):
+        to = (near, far)[step]
         return pltpu.make_async_remote_copy(
             src_ref=band.at[it, 1, :, :, pl.ds(c * part, part), :],
-            dst_ref=band.at[it, side, :, :, pl.ds(c * part, part), :],
-            send_sem=h_send.at[it, c, side // 2], recv_sem=h_recv.at[it, c, side // 2],
-            device_id={"energy": right if side == 0 else left}, device_id_type=MESH)
+            dst_ref=band.at[it, 1 + e - to, :, :, pl.ds(c * part, part), :],
+            send_sem=h_send.at[it, c, step], recv_sem=h_recv.at[it, c, step],
+            device_id={"energy": to}, device_id_type=MESH)
 
     def homeward(it, n, j):
         c, i, w = home_pieces[n]
@@ -199,7 +208,7 @@
                 onsite(it, i, 0)
                 if i == 0:
                     pl.semaphore_wait(
-                        barrier, nk - 1 + has_left.astype(jnp.int32) + has_right.astype(jnp.int32))
+                        barrier, nk - 1 + has_near.astype(jnp.int32) + has_far.astype(jnp.int32))
                 send(it, i)
         else:
             for n, (t, first, width) in enumerate(home_pieces):
@@ -224,28 +233,28 @@
                     for j in range(1, nk):
                         outward(it, n, j).wait_recv()
             if c < chunks:
-                @pl.when(has_right)
+                @pl.when(has_far)
+                def _():
+                    halo(it, c, 1).start()
+
+                @pl.when(has_near)
                 def _():
                     halo(it, c, 0).start()
-
-                @pl.when(has_left)
-                def _():
-                    halo(it, c, 2).start()
             if c > 0:
-                @pl.when(has_left)
+                @pl.when(has_near)
                 def _():
                     halo(it, c - 1, 0).wait_recv()
 
-                @pl.when(has_right)
+                @pl.when(has_far)
                 def _():
-                    halo(it, c - 1, 2).wait_recv()
+                    halo(it, c - 1, 1).wait_recv()
 
                 for n, (piece, first, width) in enumerate(home_pieces):
                     if piece == c - 1:
                         mix(it, piece, first, width)
                         for j in range(1, nk):
                             homeward(it, n, j).start()
-                        keep(it, n).start()
+                        keep(it, n).start(priority=1)
 
     for n, (t, first, width) in enumerate(home_pieces):
         arrive(ITERS - 1, n)
@@ -257,13 +266,13 @@
                 outward(it, n, j).wait_send()
                 homeward(it, n, j).wait_send()
         for c in range(chunks):
-            @pl.when(has_right)
+            @pl.when(has_near)
             def _():
                 halo(it, c, 0).wait_send()
 
-            @pl.when(has_left)
+            @pl.when(has_far)
             def _():
-                halo(it, c, 2).wait_send()
+                halo(it, c, 1).wait_send()
 
 
 def write(*refs):

time: 45.5 us -> 46 us (1.011)
  no operation moved by 1% of the time
where the time goes in v5:
time: 46 us; the launch traced here: 45.8 us
  Pallas kernels  45.1 us (98%)
  between operations  0.64 us (1%)
    pallas_call x1, Pallas kernels, body(): pl.pallas_call(functools.partial(born, ne, nk), out_shape=(pltpu.VMEM(par...  44.1 us
    pallas_call x1, Pallas kernels, body(): pl.pallas_call(write, out_shape=(result, result), in_specs=[near] * 2, ou...  1.03 us

profile of v5, /device:TPU:1, one launch (start us, length us, event | category | flops | bytes accessed | tf_op | source)
XLA Modules:
  0.0 45.8 jit_solution(3372290427367281989)
XLA Ops:
  0.6 44.1 %shard_map.77 = (bf16[3,2,3,128,128]{4,3,2,1,0:T(8,128)(2,1)S(1)}, bf16[3,2,3,128,128]{4,3,2,1,0:T(8,128)(2,1)S(1)}) custom-call(bf16[3,2,384,384]{3,2,1,0:T(8,128)(2,1)} %bitcast.8, bf16[3,2,3,128,128]{4,3,2,1,0:T(8,128)(2,1)} %bitcast.9, s32[3]{0:T(128)} %counts.1, s32[3]{0:T(128)} %offsets.1, s32[3,4,4]{2,1,0:T(4,128)} %pairs.1, f32[3,16]{1,0:T(4,128)} %table.1), custom_call_target="tpu_custom_call" | custom-call | tf_op jit(solution)/shard_map/pallas_call | solution.py:304
  44.8 1.0 %shard_map.78 = (bf16[3,2,3,128,128]{4,3,2,1,0:T(8,128)(2,1)}, bf16[3,2,3,128,128]{4,3,2,1,0:T(8,128)(2,1)}) custom-call(bf16[3,2,3,128,128]{4,3,2,1,0:T(8,128)(2,1)S(1)} %get-tuple-element.6.refs_0_, bf16[3,2,3,128,128]{4,3,2,1,0:T(8,128)(2,1)S(1)} %get-tuple-element.7.refs_1_), custom_call_target="tpu_custom_call" | custom-call | tf_op jit(solution)/shard_map/pallas_call | solution.py:332

commit v6 on v5

--- a/solution.py
+++ b/solution.py
@@ -137,12 +137,12 @@
             outward(it, n, j).start()
         mine(it, n).start(priority=1)
 
-    def halo(it, c, step):
+    def halo(it, c, i, step):
         to = (near, far)[step]
         return pltpu.make_async_remote_copy(
-            src_ref=band.at[it, 1, :, :, pl.ds(c * part, part), :],
-            dst_ref=band.at[it, 1 + e - to, :, :, pl.ds(c * part, part), :],
-            send_sem=h_send.at[it, c, step], recv_sem=h_recv.at[it, c, step],
+            src_ref=band.at[it, 1, i, :, pl.ds(c * part, part), :],
+            dst_ref=band.at[it, 1 + e - to, i, :, pl.ds(c * part, part), :],
+            send_sem=h_send.at[it, c, i, step], recv_sem=h_recv.at[it, c, i, step],
             device_id={"energy": to}, device_id_type=MESH)
 
     def homeward(it, n, j):
@@ -227,27 +227,31 @@
         if it == 0:
             prepare()
         for c in range(chunks + 1):
-            for n, (piece, _, _) in enumerate(out_pieces):
+            for n, (piece, first, width) in enumerate(out_pieces):
                 if piece == c:
                     mine(it, n).wait()
                     for j in range(1, nk):
                         outward(it, n, j).wait_recv()
-            if c < chunks:
-                @pl.when(has_far)
-                def _():
-                    halo(it, c, 1).start()
-
-                @pl.when(has_near)
-                def _():
-                    halo(it, c, 0).start()
+
+                    @pl.when(has_far)
+                    def _():
+                        for i in range(first, first + width):
+                            halo(it, c, i, 1).start()
+
+                    @pl.when(has_near)
+                    def _():
+                        for i in range(first, first + width):
+                            halo(it, c, i, 0).start()
             if c > 0:
                 @pl.when(has_near)
                 def _():
-                    halo(it, c - 1, 0).wait_recv()
+                    for i in range(energies):
+                        halo(it, c - 1, i, 0).wait_recv()
 
                 @pl.when(has_far)
                 def _():
-                    halo(it, c - 1, 1).wait_recv()
+                    for i in range(energies):
+                        halo(it, c - 1, i, 1).wait_recv()
 
                 for n, (piece, first, width) in enumerate(home_pieces):
                     if piece == c - 1:
@@ -268,11 +272,13 @@
         for c in range(chunks):
             @pl.when(has_near)
             def _():
-                halo(it, c, 0).wait_send()
+                for i in range(energies):
+                    halo(it, c, i, 0).wait_send()
 
             @pl.when(has_far)
             def _():
-                halo(it, c, 1).wait_send()
+                for i in range(energies):
+                    halo(it, c, i, 1).wait_send()
 
 
 def write(*refs):
@@ -320,8 +326,8 @@
             dma((ITERS, 2, pieces)),
             dma((ITERS, pieces, nk)),
             dma((ITERS, pieces, nk)),
-            dma((ITERS, chunks, 2)),
-            dma((ITERS, chunks, 2)),
+            dma((ITERS, chunks, energies, 2)),
+            dma((ITERS, chunks, energies, 2)),
             dma((ITERS, pieces, nk)),
             dma((ITERS, pieces, nk)),
         ],

time: 46 us -> 44.9 us (0.976)
  Pallas kernels: 45.1 us -> 44.1 us
    pallas_call x1, Pallas kernels: 44.1 us -> 43.1 us  [body(): pl.pallas_call(functools.partial(born, ne, nk), out_shape=(pltpu.VMEM(par...]
where the time goes in v6:
time: 44.9 us; the launch traced here: 44.8 us
  Pallas kernels  44.1 us (98%)
  between operations  0.64 us (1%)
    pallas_call x1, Pallas kernels, body(): pl.pallas_call(functools.partial(born, ne, nk), out_shape=(pltpu.VMEM(par...  43.1 us
    pallas_call x1, Pallas kernels, body(): pl.pallas_call(write, out_shape=(result, result), in_specs=[near] * 2, ou...  1.03 us

profile of v6, /device:TPU:1, one launch (start us, length us, event | category | flops | bytes accessed | tf_op | source)
XLA Modules:
  0.0 44.8 jit_solution(15071918684103854597)
XLA Ops:
  0.6 43.1 %shard_map.77 = (bf16[3,2,3,128,128]{4,3,2,1,0:T(8,128)(2,1)S(1)}, bf16[3,2,3,128,128]{4,3,2,1,0:T(8,128)(2,1)S(1)}) custom-call(bf16[3,2,384,384]{3,2,1,0:T(8,128)(2,1)} %bitcast.8, bf16[3,2,3,128,128]{4,3,2,1,0:T(8,128)(2,1)} %bitcast.9, s32[3]{0:T(128)} %counts.1, s32[3]{0:T(128)} %offsets.1, s32[3,4,4]{2,1,0:T(4,128)} %pairs.1, f32[3,16]{1,0:T(4,128)} %table.1), custom_call_target="tpu_custom_call" | custom-call | tf_op jit(solution)/shard_map/pallas_call | solution.py:310
  43.7 1.0 %shard_map.78 = (bf16[3,2,3,128,128]{4,3,2,1,0:T(8,128)(2,1)}, bf16[3,2,3,128,128]{4,3,2,1,0:T(8,128)(2,1)}) custom-call(bf16[3,2,3,128,128]{4,3,2,1,0:T(8,128)(2,1)S(1)} %get-tuple-element.6.refs_0_, bf16[3,2,3,128,128]{4,3,2,1,0:T(8,128)(2,1)S(1)} %get-tuple-element.7.refs_1_), custom_call_target="tpu_custom_call" | custom-call | tf_op jit(solution)/shard_map/pallas_call | solution.py:338

commit v7 on v6

--- a/solution.py
+++ b/solution.py
@@ -1,5 +1,4 @@
 import functools
-import math
 
 import jax
 import jax.numpy as jnp
@@ -40,14 +39,8 @@
     home_pieces = [(c, 0, energies) for c in range(chunks - 1)]
     home_pieces += [(chunks - 1, i, 1) for i in range(energies)]
 
-    side = math.isqrt(nk)
-
     def peer(j):
-        if side * side != nk:
-            return lax.rem(me + j, nk)
-        high, low = j // side, j % side
-        high, low = high + odd * (low - high), low + odd * (high - low)
-        return lax.rem(me // side + high, side) * side + lax.rem(me % side + low, side)
+        return lax.rem(me + j, nk)
 
     barrier = pltpu.get_barrier_semaphore()
     for j in range(1, nk):

time: 44.9 us -> 44.5 us (level)
  Pallas kernels: 44.1 us -> 43.6 us
    pallas_call x1, Pallas kernels: 43.1 us -> 42.6 us  [body(): pl.pallas_call(functools.partial(born, ne, nk), out_shape=(pltpu.VMEM(par...]
where the time goes in v7:
time: 44.5 us; the launch traced here: 44.3 us
  Pallas kernels  43.6 us (98%)
  between operations  0.64 us (1%)
    pallas_call x1, Pallas kernels, body(): pl.pallas_call(functools.partial(born, ne, nk), out_shape=(pltpu.VMEM(par...  42.6 us
    pallas_call x1, Pallas kernels, body(): pl.pallas_call(write, out_shape=(result, result), in_specs=[near] * 2, ou...  1.03 us

profile of v7, /device:TPU:1, one launch (start us, length us, event | category | flops | bytes accessed | tf_op | source)
XLA Modules:
  0.0 44.3 jit_solution(7667979334745150791)
XLA Ops:
  0.6 42.6 %shard_map.77 = (bf16[3,2,3,128,128]{4,3,2,1,0:T(8,128)(2,1)S(1)}, bf16[3,2,3,128,128]{4,3,2,1,0:T(8,128)(2,1)S(1)}) custom-call(bf16[3,2,384,384]{3,2,1,0:T(8,128)(2,1)} %bitcast.8, bf16[3,2,3,128,128]{4,3,2,1,0:T(8,128)(2,1)} %bitcast.9, s32[3]{0:T(128)} %counts.1, s32[3]{0:T(128)} %offsets.1, s32[3,4,4]{2,1,0:T(4,128)} %pairs.1, f32[3,16]{1,0:T(4,128)} %table.1), custom_call_target="tpu_custom_call" | custom-call | tf_op jit(solution)/shard_map/pallas_call | solution.py:303
  43.2 1.0 %shard_map.78 = (bf16[3,2,3,128,128]{4,3,2,1,0:T(8,128)(2,1)}, bf16[3,2,3,128,128]{4,3,2,1,0:T(8,128)(2,1)}) custom-call(bf16[3,2,3,128,128]{4,3,2,1,0:T(8,128)(2,1)S(1)} %get-tuple-element.6.refs_0_, bf16[3,2,3,128,128]{4,3,2,1,0:T(8,128)(2,1)S(1)} %get-tuple-element.7.refs_1_), custom_call_target="tpu_custom_call" | custom-call | tf_op jit(solution)/shard_map/pallas_call | solution.py:331
